TPU v7x, 32 devices: a whole 2x2x4 slice. The times are simulated.
32 devices in a mesh: layer: 8 (over z, x), dp: 4 (over y, core).
Axes of the slice: x: 2, y: 2, z: 4, core: 2. Of those that a mesh axis runs over, the one named last changes fastest.
Arguments:
- images: float32 [4, 56, 56, 128], P('dp'), may hold values from -6 to 6
- kernels: bfloat16 [24, 1152, 128], P('layer'), may hold values from -0.1875 to 0.1875
- damping: float32 [24, 128], P('layer'), may hold values from 0.02 to 4
- cotangent: float32 [4, 56, 56, 128], P('dp'), may hold values from -6 to 6
Outputs:
- slab_ends: float32 [8, 4, 56, 56, 128], P('layer', 'dp')
- coarse_ends: float32 [8, 4, 56, 56, 128], P('layer', 'dp')
- adjoint_starts: float32 [8, 4, 56, 56, 128], P('layer', 'dp')
- adjoint_coarse_starts: float32 [8, 4, 56, 56, 128], P('layer', 'dp')
- gradients: float32 [24, 1152, 128], P('layer')
All inputs are finite; a program needn't handle non-finite values.
Results may differ from a plain program's by a relative error of at most 0.0054.
Values sent between devices are 32-bit elements; how exact they have to be, the bound alone decides.
No kernel may reach another device: no remote copies, remote signals or barrier semaphores. Data moves between devices by JAX's collectives and lax.ppermute only.
A program may use at most 256 MiB of HBM per device.

v0:
```python
import jax
import jax.numpy as jnp
from jax import lax
from jax.sharding import PartitionSpec as P

STEP = 0.125


def from_behind(shard, axis, by):
    devices = lax.axis_size(axis)
    pairs = [(i, i + by) for i in range(devices) if 0 <= i + by < devices]
    return lax.ppermute(shard, axis, pairs)


def patches(field):
    side = field.shape[1]
    padded = jnp.pad(field, ((0, 0), (1, 1), (1, 1), (0, 0)))
    pieces = [
        padded[:, row_off : row_off + side, col_off : col_off + side, :]
        for row_off in range(3)
        for col_off in range(3)
    ]
    return jnp.concatenate(pieces, axis=-1).reshape(-1, 9 * field.shape[3])


def advance(current, kernel, decay):
    columns = patches(current.astype(jnp.bfloat16))
    preact = jnp.dot(columns, kernel, preferred_element_type=jnp.float32).reshape(current.shape)
    activation = jnp.tanh(preact)
    return (current + STEP * (activation - decay * current), activation, columns)


def retreat(adjoint, activation, kernel_back, decay):
    scaled = (STEP * (1.0 - activation * activation) * adjoint).astype(jnp.bfloat16)
    back_term = jnp.dot(patches(scaled), kernel_back, preferred_element_type=jnp.float32).reshape(
        adjoint.shape
    )
    return (adjoint - STEP * decay * adjoint + back_term, scaled)


def flipped(kernel):
    channels = kernel.shape[1]
    blocks = kernel.reshape(9, channels, channels)[::-1]
    return jnp.swapaxes(blocks, 1, 2).reshape(9 * channels, channels)


def coarse(kernel, decay, layers):
    channels = kernel.shape[1]
    tap_sum = jnp.sum(kernel.astype(jnp.float32).reshape(9, channels, channels), axis=0)
    return jnp.diag(1.0 - layers * STEP * decay) + layers * STEP * tap_sum


def high_dot(left, right):
    return jnp.dot(left, right, precision=lax.Precision.HIGHEST, preferred_element_type=jnp.float32)


def transform(current, matrix):
    return high_dot(current.reshape(-1, matrix.shape[0]), matrix).reshape(current.shape)


def sweep(current, kernel_set, decay_set):
    for layer_id in range(kernel_set.shape[0]):
        current, _, _ = advance(current, kernel_set[layer_id], decay_set[layer_id])
    return current


def sweep_back(adjoint, act_list, back_list, decay_set):
    for layer_id in reversed(range(len(act_list))):
        adjoint, _ = retreat(adjoint, act_list[layer_id], back_list[layer_id], decay_set[layer_id])
    return adjoint


def relay_chain(seed, offset, matrix, backward):
    full_shape = seed.shape
    channels = full_shape[-1]
    seed_rows = seed.reshape(-1, channels)
    term_rows = offset.reshape(-1, channels)
    pieces = 16
    piece_rows = seed_rows.shape[0] // pieces
    span_size = lax.axis_size("layer")
    position = lax.axis_index("layer")
    order_pos = span_size - 1 - position if backward else position

    def advance_block(step_id, state_pair):
        outgoing, collected = state_pair
        if backward:
            incoming = from_behind(outgoing, "layer", -1)
        else:
            incoming = from_behind(outgoing, "layer", 1)
        block_id = step_id - order_pos
        inside = (block_id >= 0) & (block_id < pieces)
        first_row = jnp.clip(block_id, 0, pieces - 1) * piece_rows
        own_rows = lax.dynamic_slice_in_dim(seed_rows, first_row, piece_rows, 0)
        entering = jnp.where(order_pos == 0, own_rows, incoming)
        leaving = high_dot(entering, matrix) + lax.dynamic_slice_in_dim(
            term_rows, first_row, piece_rows, 0
        )
        old_rows = lax.dynamic_slice_in_dim(collected, first_row, piece_rows, 0)
        collected = lax.dynamic_update_slice_in_dim(
            collected, jnp.where(inside, entering, old_rows), first_row, 0
        )
        return (leaving, collected)

    initial = (jnp.zeros((piece_rows, channels), jnp.float32), jnp.zeros_like(seed_rows))
    _, collected = lax.fori_loop(0, span_size + pieces - 1, advance_block, initial)
    return collected.reshape(full_shape)


def coarse_chain(seed, offset, matrix, backward):
    return relay_chain(seed, offset, matrix, backward)


def per_device(images, kernels, damping, cotangent):
    slab = kernels.shape[0]
    channels = images.shape[3]
    span_size = lax.axis_size("layer")
    position = lax.axis_index("layer")
    back_list = [flipped(kernels[layer_id]) for layer_id in range(slab)]
    matrix = coarse(kernels[0], damping[0], slab)
    slab_end = sweep(images, kernels, damping)
    arriving = from_behind(slab_end, "layer", 1)
    start_states = jnp.where(position == 0, images, arriving)
    offset = sweep(start_states, kernels, damping) - transform(start_states, matrix)
    begins = coarse_chain(images, offset, matrix, False)
    coarse_out = transform(begins, matrix) + offset
    current = begins
    act_list = []
    column_list = []
    for layer_id in range(slab):
        current, activation, columns = advance(current, kernels[layer_id], damping[layer_id])
        act_list.append(activation)
        column_list.append(columns)
    head_states = sweep_back(cotangent, act_list, back_list, damping)
    arriving_back = from_behind(head_states, "layer", -1)
    top_states = jnp.where(position == span_size - 1, cotangent, arriving_back)
    back_offset = sweep_back(top_states, act_list, back_list, damping) - transform(
        top_states, matrix.T
    )
    adjoint_state = coarse_chain(cotangent, back_offset, matrix.T, True)
    adjoint_out = transform(adjoint_state, matrix.T) + back_offset
    grad_list = [None] * slab
    for layer_id in reversed(range(slab)):
        adjoint_state, scaled = retreat(
            adjoint_state, act_list[layer_id], back_list[layer_id], damping[layer_id]
        )
        local_grad = lax.dot_general(
            column_list[layer_id],
            scaled.reshape(-1, channels),
            (((0,), (0,)), ((), ())),
            preferred_element_type=jnp.float32,
        )
        local_grad = lax.psum(local_grad, "dp")
        grad_list[layer_id] = local_grad
    stacked = jnp.stack(grad_list)
    return (current[None], coarse_out[None], adjoint_state[None], adjoint_out[None], stacked)


def solution(mesh):
    in_specs = (
        P("dp", None, None, None),
        P("layer", None, None),
        P("layer", None),
        P("dp", None, None, None),
    )
    out_specs = (
        P("layer", "dp", None, None, None),
        P("layer", "dp", None, None, None),
        P("layer", "dp", None, None, None),
        P("layer", "dp", None, None, None),
        P("layer", None, None),
    )
    return jax.shard_map(
        per_device, mesh=mesh, in_specs=in_specs, out_specs=out_specs, check_vma=False
    )
```

profile of v0, /device:TPU:0, one launch (start us, length us, event | category | flops | bytes accessed | tf_op | source)
XLA Modules:
  0.0 795.9 jit_solution(15205044323870152683)
XLA Ops:
  26.7 6.0 collective-permute-start.2
  42.1 24.1 %collective-permute-done.2 = f32[1,56,56,128]{3,2,1,0:T(8,128)} collective-permute-done((f32[1,56,56,128]{3,2,1,0:T(8,128)}, f32[1,56,56,128]{3,2,1,0:T(8,128)}, u32[]{:S(2)}, u32[]{:S(2)}) %collective-permute-start.2) | collective-permute-done | bytes 1605664 | tf_op jit(solution)/shard_map/ppermute | solution.py:12
  77.6 13.1 %slice_dynamic-update-slice_fusion.52 = bf16[1,56,56,1152]{3,2,1,0:T(8,128)(2,1)S(1)} fusion(bf16[1,56,56,1152]{3,2,1,0:T(8,128)(2,1)S(1)} %slice_dynamic-update-slice_fusion.53, bf16[1,56,56,128]{3,2,1,0:T(8,128)(2,1)S(1)} %get-tuple-element.478), kind=kLoop, calls=%fused_computation.210 | loop fusion | bytes 1605632
  97.6 254.8 %while.34 = (s32[]{:T(128)}, f32[196,128]{1,0:T(8,128)}, f32[3136,128]{1,0:T(8,128)S(1)}, pred[]{:T(512)}, s32[]{:T(128)}, /*index=5*/f32[3136,128]{1,0:T(8,128)...) while((s32[]{:T(128)}, f32[196,128]{1,0:T(8,128)}, ...), condition=%wide.region_2.3_spmd.clone, body=%wide.region_1.2_spmd.clone.sunk | while | flops 38660616 | bytes 1676585 | solution.py:105
  97.6 5.8 collective-permute-start
  405.5 5.9 collective-permute-done.3
  432.0 265.2 %while.35 = (s32[]{:T(128)}, f32[196,128]{1,0:T(8,128)S(1)}, f32[3136,128]{1,0:T(8,128)}, pred[]{:T(512)}, s32[]{:T(128)}, /*index=5*/f32[3136,128]{1,0:T(8,128)...) while((s32[]{:T(128)}, f32[196,128]{1,0:T(8,128)S(1)}, ...), condition=%wide.region_4.5_spmd.clone, body=%wide.region_3.4_spmd.clone.sunk | while | flops 38660616 | bytes 1677096 | solution.py:105
  433.3 6.9 collective-permute-done.1
  445.4 6.1 collective-permute-done.1
  456.9 6.6 collective-permute-done.1
  468.7 7.0 collective-permute-done.1
  481.0 5.9 collective-permute-done.1
  492.1 6.1 collective-permute-done.1
  503.5 6.1 collective-permute-done.1
  515.0 6.1 collective-permute-done.1
  526.4 6.1 collective-permute-done.1
  537.8 6.1 collective-permute-done.1
  549.2 6.1 collective-permute-done.1
  560.6 6.4 collective-permute-done.1
  572.3 7.2 collective-permute-done.1
  584.8 5.9 collective-permute-done.1
  595.9 6.1 collective-permute-done.1
  607.3 6.1 collective-permute-done.1
  618.7 6.1 collective-permute-done.1
  630.2 6.1 collective-permute-done.1
  641.6 6.1 collective-permute-done.1
  653.0 6.1 collective-permute-done.1
  664.4 6.1 collective-permute-done.1
  675.8 6.1 collective-permute-done.1
  687.2 6.1 collective-permute-done.1
  740.5 6.5 fusion.51
  747.0 39.0 %all-reduce.21.cloned.1.call-done = (f32[1,1152,128]{2,1,0:T(8,128)}, f32[1,1152,128]{2,1,0:T(8,128)}, f32[1,1152,128]{2,1,0:T(8,128)}) async-done(((f32[1,1152,128]{2,1,0:T(8,128)}, f32[1,1152,128]{2,1,0:T(8,128)}, f32[1,1152,128]{2,1,0:T(8,128)}), (f32[1,1152,128]{2,1,0:T(8,128)}, f32[1,1152,128]{2,1,0:T(8,128)}, f32[1,1152,128]{2,1,0:T(8,128)})) %all-reduce.21.cloned.1.call-update) | async-done | bytes 1769488 | tf_op jit(solution)/shard_map/psum | solution.py:152
  (558 shorter events, 533.4 us)
Async XLA Ops:
  7.2 778.8 %all-reduce.21.cloned.1.call-start = ((), (), s32[]{:S(2)}) async-start(), calls=%async_computation | async-start | bytes 3538944 | tf_op jit(solution)/shard_map/psum | solution.py:152
  26.7 39.5 %collective-permute-start.2 = (f32[1,56,56,128]{3,2,1,0:T(8,128)}, f32[1,56,56,128]{3,2,1,0:T(8,128)}, u32[]{:S(2)}, u32[]{:S(2)}) collective-permute-start(f32[1,56,56,128]{3,2,1,0:T(8,128)} %fusion.69), channel_id=1, source_target_pairs={{0,4},{4,8},{8,12},{12,16},{16,20},{20,24},{24,28},{1,5},{5,9},{9,... | collective-permute-start | bytes 4816904 | tf_op jit(solution)/shard_map/ppermute | solution.py:12
  97.6 8.0 %collective-permute-start = (f32[196,128]{1,0:T(8,128)S(1)}, f32[196,128]{1,0:T(8,128)S(1)}, u32[]{:S(2)}, u32[]{:S(2)}) collective-permute-start(f32[196,128]{1,0:T(8,128)S(1)} %broadcast_select_fusion.8), channel_id=1, source_target_pairs={{0,4},{4,8},{8,12},{12,16},{16,20},{20,24},{24,28},{1,5},{5,9},{9,... | collective-permute-start | bytes 301064 | tf_op jit(solution)/shard_map/while/body/eval_jaxpr/ppermute | solution.py:12
  153.0 7.5 collective-permute-start
  175.2 8.3 %collective-permute-start = (f32[196,128]{1,0:T(8,128)S(1)}, f32[196,128]{1,0:T(8,128)S(1)}, u32[]{:S(2)}, u32[]{:S(2)}) collective-permute-start(f32[196,128]{1,0:T(8,128)S(1)} %broadcast_select_fusion.8), channel_id=1, source_target_pairs={{0,4},{4,8},{8,12},{12,16},{16,20},{20,24},{24,28},{1,5},{5,9},{9,... | collective-permute-start | bytes 301064 | tf_op jit(solution)/shard_map/while/body/eval_jaxpr/ppermute | solution.py:12
  187.2 7.7 collective-permute-start
  198.5 7.5 collective-permute-start
  209.7 7.5 collective-permute-start
  220.9 7.4 collective-permute-start
  243.1 7.5 collective-permute-start
  265.3 7.5 collective-permute-start
  276.2 8.6 %collective-permute-start = (f32[196,128]{1,0:T(8,128)S(1)}, f32[196,128]{1,0:T(8,128)S(1)}, u32[]{:S(2)}, u32[]{:S(2)}) collective-permute-start(f32[196,128]{1,0:T(8,128)S(1)} %broadcast_select_fusion.8), channel_id=1, source_target_pairs={{0,4},{4,8},{8,12},{12,16},{16,20},{20,24},{24,28},{1,5},{5,9},{9,... | collective-permute-start | bytes 301064 | tf_op jit(solution)/shard_map/while/body/eval_jaxpr/ppermute | solution.py:12
  298.9 7.8 collective-permute-start
  386.7 24.7 %collective-permute-start.3 = (f32[1,56,56,128]{3,2,1,0:T(8,128)S(1)}, f32[1,56,56,128]{3,2,1,0:T(8,128)S(1)}, u32[]{:S(2)}, u32[]{:S(2)}) collective-permute-start(f32[1,56,56,128]{3,2,1,0:T(8,128)S(1)} %fusion.43), channel_id=1, source_target_pairs={{4,0},{8,4},{12,8},{16,12},{20,16},{24,20},{28,24},{5,1},{9,5},{13... | collective-permute-start | bytes 4816904 | tf_op jit(solution)/shard_map/ppermute | solution.py:12
  432.0 8.2 %collective-permute-start.1 = (f32[196,128]{1,0:T(8,128)S(1)}, f32[196,128]{1,0:T(8,128)S(1)}, u32[]{:S(2)}, u32[]{:S(2)}) collective-permute-start(f32[196,128]{1,0:T(8,128)S(1)} %broadcast_select_fusion.9), channel_id=1, source_target_pairs={{4,0},{8,4},{12,8},{16,12},{20,16},{24,20},{28,24},{5,1},{9,5},{13... | collective-permute-start | bytes 301064 | tf_op jit(solution)/shard_map/while/body/eval_jaxpr/ppermute | solution.py:12
  444.1 7.5 collective-permute-start.1
  455.5 7.9 collective-permute-start.1
  467.4 8.3 %collective-permute-start.1 = (f32[196,128]{1,0:T(8,128)S(1)}, f32[196,128]{1,0:T(8,128)S(1)}, u32[]{:S(2)}, u32[]{:S(2)}) collective-permute-start(f32[196,128]{1,0:T(8,128)S(1)} %broadcast_select_fusion.9), channel_id=1, source_target_pairs={{4,0},{8,4},{12,8},{16,12},{20,16},{24,20},{28,24},{5,1},{9,5},{13... | collective-permute-start | bytes 301064 | tf_op jit(solution)/shard_map/while/body/eval_jaxpr/ppermute | solution.py:12
  490.8 7.5 collective-permute-start.1
  502.2 7.5 collective-permute-start.1
  513.6 7.5 collective-permute-start.1
  525.0 7.5 collective-permute-start.1
  536.5 7.4 collective-permute-start.1
  547.9 7.5 collective-permute-start.1
  559.3 7.7 collective-permute-start.1
  571.0 8.5 %collective-permute-start.1 = (f32[196,128]{1,0:T(8,128)S(1)}, f32[196,128]{1,0:T(8,128)S(1)}, u32[]{:S(2)}, u32[]{:S(2)}) collective-permute-start(f32[196,128]{1,0:T(8,128)S(1)} %broadcast_select_fusion.9), channel_id=1, source_target_pairs={{4,0},{8,4},{12,8},{16,12},{20,16},{24,20},{28,24},{5,1},{9,5},{13... | collective-permute-start | bytes 301064 | tf_op jit(solution)/shard_map/while/body/eval_jaxpr/ppermute | solution.py:12
  594.6 7.5 collective-permute-start.1
  606.0 7.4 collective-permute-start.1
  617.4 7.5 collective-permute-start.1
  628.8 7.4 collective-permute-start.1
  640.2 7.5 collective-permute-start.1
  663.1 7.5 collective-permute-start.1
  (47 other events, 343.5 us)
Sparse Core Ops, SparseCore 0:
  736.5 49.3 all-reduce.20
where the time goes:
time: 810 us; the launch traced here: 796 us
  waiting for transfers between devices  266 us (33%)
  starting transfers between devices  158 us (20%)
  local copies, waits for them, and re-layouts  150 us (19%)
  matrix products  146 us (18%)
  other arithmetic  58.8 us (7%)
  between operations  16 us (2%)
    ppermute x48, waiting for transfers between devices, from_behind(): return lax.ppermute(shard, axis, pairs)  227 us
    ppermute x48, starting transfers between devices, from_behind(): return lax.ppermute(shard, axis, pairs)  158 us
    dot_general x50, matrix products, high_dot(): jnp.dot(left, right, precision=lax.Precision.HIGHEST, preferred_element_t...  86.2 us
    unnamed x227, local copies, waits for them, and re-layouts  77.4 us
    dynamic_update_slice x46, local copies, waits for them, and re-layouts, advance_block(): lax.dynamic_update_slice_in_dim(collected, jnp.where(inside, entering, ol...  54.4 us
    psum x1, waiting for transfers between devices, per_device(): local_grad = lax.psum(local_grad, 'dp')  39 us
    dot_general x9, matrix products, retreat(): jnp.dot(patches(scaled), kernel_back, preferred_element_type=jnp.float32)  27.8 us
    dot_general x9, matrix products, advance(): jnp.dot(columns, kernel, preferred_element_type=jnp.float32)  23.2 us
  transfers between devices with their start and end apart: 49, of which 49 were waited for; matrix products, arithmetic and copies ran while one was open for 5% of the time, Pallas kernels for 0%

commit v1 on v0

v1 whole, which is shorter than its diff:
```python
import functools

import jax
import jax.numpy as jnp
from jax import lax
from jax.experimental import pallas as pl
from jax.experimental.pallas import tpu as pltpu
from jax.sharding import PartitionSpec as P

STEP = 0.125
F32 = jnp.float32
BF16 = jnp.bfloat16
BLOCK_PAIRS = 14
GROUP = 4
TOGETHER = 1


def wide_of(side):
    return -(-(side + 1) // 16) * 16


def columns_shape(field):
    pairs, _, side, channels = field
    return (pairs + 1, 2, wide_of(side), 3 * channels)


def per_block(pairs, body, together=1):
    count = BLOCK_PAIRS if pairs % BLOCK_PAIRS == 0 else 1
    together = together if pairs // count % together == 0 else 1

    def step(block, carry):
        for number in range(together):
            body((block * together + number) * count, count)
        return carry

    lax.fori_loop(0, pairs // count // together, step, 0)


def clear_borders(columns):
    edge = jnp.zeros(columns.shape[2:], BF16)
    columns[0, 0] = edge
    columns[columns.shape[0] - 1, 1] = edge


def put_columns(columns, first, odd, rows):
    count, side, channels = rows.shape
    wide = columns.shape[2]
    here = jnp.concatenate([rows, jnp.zeros((count, wide - side, channels), F32)], axis=1)
    left = pltpu.roll(here, 1, 1)
    right = pltpu.roll(here, wide - 1, 1)
    columns[pl.ds(first + odd, count), 1 - odd] = jnp.concatenate([left, here, right], axis=2).astype(BF16)


def spread(paired, kernel):
    taps, channels = kernel.shape
    third = taps // 3
    blank = jnp.zeros((third, channels), BF16)
    paired[0:taps, 0:channels] = kernel
    paired[taps : taps + third, 0:channels] = blank
    paired[0:third, channels : 2 * channels] = blank
    paired[third : taps + third, channels : 2 * channels] = kernel


def convolve(columns, paired, first, count, side):
    _, _, wide, depth = columns.shape
    channels = depth // 3
    pieces = [
        columns[pl.ds(first, count), 0],
        columns[pl.ds(first, count), 1],
        columns[pl.ds(first + 1, count), 0],
        columns[pl.ds(first + 1, count), 1],
    ]
    left = jnp.concatenate([piece.reshape(count * wide, depth) for piece in pieces], axis=1)
    both = jnp.dot(left, paired[...], preferred_element_type=F32)
    return [
        both[:, odd * channels : (odd + 1) * channels].reshape(count, wide, channels)[:, :side]
        for odd in range(2)
    ]


def split_dot(left, matrix):
    high = left.astype(BF16)
    low = (left - high.astype(F32)).astype(BF16)
    m_high = matrix.astype(BF16)
    m_low = (matrix - m_high.astype(F32)).astype(BF16)
    return jnp.dot(
        jnp.concatenate([high, low, high], axis=1),
        jnp.concatenate([m_high, m_high, m_low], axis=0),
        preferred_element_type=F32,
    )


def transform_rows(rows, matrix):
    count, side, channels = rows.shape
    return split_dot(rows.reshape(count * side, channels), matrix).reshape(rows.shape)


def fill_forward(state, columns):
    def fill(first, count):
        for odd in range(2):
            put_columns(columns, first, odd, state[pl.ds(first, count), odd])

    per_block(state.shape[0], fill)


def forward_layer(current, columns, paired, rate, store):
    pairs, _, side, _ = current.shape
    decay = rate.reshape(1, 1, -1)

    def block(first, count):
        rows = pl.ds(first, count)
        for odd, preact in enumerate(convolve(columns, paired, first, count, side)):
            activation = jnp.tanh(preact)
            here = current[rows, odd]
            store(rows, first, odd, here + STEP * (activation - decay * here), activation)

    per_block(pairs, block, TOGETHER)


def scaled_rows(adjoint, activation):
    return STEP * (1.0 - activation * activation) * adjoint


def fill_backward(state, activation, columns):
    def fill(first, count):
        rows = pl.ds(first, count)
        for odd in range(2):
            put_columns(columns, first, odd, scaled_rows(state[rows, odd], activation[rows, odd]))

    per_block(state.shape[0], fill)


def backward_layer(current, columns, paired, rate, store):
    pairs, _, side, _ = current.shape
    decay = rate.reshape(1, 1, -1)

    def block(first, count):
        rows = pl.ds(first, count)
        for odd, back_term in enumerate(convolve(columns, paired, first, count, side)):
            here = current[rows, odd]
            store(rows, first, odd, here - STEP * decay * here + back_term)

    per_block(pairs, block, TOGETHER)


def params(mebibytes=40):
    return pltpu.CompilerParams(vmem_limit_bytes=mebibytes * 1024 * 1024)


def cost(field, products, extra=0):
    pairs, _, side, channels = field
    flops = products * 2 * pairs * 2 * side * channels * channels * 9
    return pl.CostEstimate(flops=flops, bytes_accessed=1000000 + extra, transcendentals=0)


def small_cost(shape, products):
    rows, channels = flat_of(shape)
    flops = products * 2 * rows * 3 * channels * channels
    return pl.CostEstimate(flops=flops, bytes_accessed=6 * 4 * rows * channels, transcendentals=0)


ANY = pl.BlockSpec(memory_space=pl.ANY)
VMEM = pl.BlockSpec(memory_space=pltpu.VMEM)
SMEM = pl.BlockSpec(memory_space=pltpu.SMEM)

def chunks_of(quarter):
    return (quarter,)


POSITION, FORWARD, BACKWARD, CHUNK, FORWARD_HEAD, BACKWARD_HEAD, SIZE = range(7)


def load(pairs_of_refs, sems, base):
    copies = []
    for number, (source, target) in enumerate(pairs_of_refs):
        copies.append(pltpu.make_async_copy(source, target, sems.at[base + number]))
        copies[-1].start()
    return copies


def finish(copies):
    for copy in copies:
        copy.wait()


def scratch_of(field, buffers):
    shape = columns_shape(field)
    return [pltpu.VMEM(shape, BF16)] * buffers + [pltpu.VMEM((4 * shape[3], 2 * field[3]), BF16)]


def join_halves(whole, low, high, half):
    rows = whole.shape[0] // 2
    whole[pl.ds(half * rows, rows)] = low[0:rows].astype(BF16)
    whole[pl.ds((1 - half) * rows, rows)] = high[0:rows].astype(BF16)


def layer_kernel(place, field, low, high, result, columns, paired, whole):
    half = lax.rem(place[CHUNK], 2)
    join_halves(whole, low, high, half)
    spread(paired, whole[...])
    rows = whole.shape[0] // 2
    clear_borders(columns)
    fill_forward(field, columns)

    def store(where, first, odd, following, activation):
        result[where, odd] = following

    forward_layer(field, columns, paired, low[rows : rows + 1], store)


def fetched_layer(place, field, low, high):
    rows, channels = low.shape[0] - 8, low.shape[1]
    return pl.pallas_call(
        layer_kernel,
        out_shape=jax.ShapeDtypeStruct(field.shape, F32),
        in_specs=[SMEM] + [VMEM] * 3,
        out_specs=VMEM,
        scratch_shapes=scratch_of(field.shape, 1) + [pltpu.VMEM((2 * rows, channels), BF16)],
        compiler_params=params(),
        cost_estimate=cost(field.shape, 1),
    )(place, field, low, high)


def piece_refs(member, group, chunks, field, shift, chunk, forward_shift):
    quarter = field.shape[0] // group
    offset = sum(chunks[:chunk])
    turn = member + shift if forward_shift else member - shift + group
    return field.at[pl.ds(lax.rem(turn, group) * quarter + offset, chunks[chunk])]


def send_out(member, group, chunks, field, outs, sems, base):
    copies = []
    for chunk in range(len(chunks)):
        for shift in range(group):
            number = chunk * group + shift
            source = piece_refs(member, group, chunks, field, shift, chunk, True)
            copies.append(pltpu.make_async_copy(source, outs[number], sems.at[base + number]))
            copies[-1].start()
    return copies


def bring_in(member, group, chunks, pieces, field, sems, base):
    copies = []
    for chunk in range(len(chunks)):
        for shift in range(group):
            number = chunk * group + shift
            target = piece_refs(member, group, chunks, field, shift, chunk, False)
            copies.append(pltpu.make_async_copy(pieces[number], target, sems.at[base + number]))
            copies[-1].start()
    return copies


def piece_shapes(field, group, chunks):
    return [jax.ShapeDtypeStruct((count,) + field[1:], F32) for count in chunks for _ in range(group)]


def offset_kernel(layers, group, chunks, place, images_hbm, field, low, high, kernels_hbm, decay, matrix, *refs):
    count_pieces = group * len(chunks)
    out, pieces = refs[0], refs[1 : 1 + count_pieces]
    images, kernels, starts, offset, now, later, paired, whole, sems = refs[1 + count_pieces :]
    pairs = offset.shape[0]
    loads = load([(images_hbm, images), (kernels_hbm, kernels)], sems, 0)
    half = lax.rem(place[CHUNK], 2)
    first_slab = place[POSITION] == 0
    join_halves(whole, low, high, half)
    spread(paired, whole[...])
    rows = whole.shape[0] // 2
    clear_borders(now)
    clear_borders(later)
    fill_forward(field, now)
    loads[0].wait()

    def store_start(where, first, odd, following, activation):
        begin = jnp.where(first_slab, images[where, odd], following)
        starts[where, odd] = begin
        put_columns(later, first, odd, begin)

    forward_layer(field, now, paired, low[rows : rows + 1], store_start)
    loads[1].wait()
    for layer in range(layers):
        now, later = later, now
        spread(paired, kernels[layer])

        def store(where, first, odd, following, activation, last=layer == layers - 1, target=later):
            if last:
                following = following - transform_rows(starts[where, odd], matrix[...])
            else:
                put_columns(target, first, odd, following)
            offset[where, odd] = following

        forward_layer(starts if layer == 0 else offset, now, paired, decay[layer : layer + 1], store)

    copies = send_out(place[FORWARD], group, chunks, offset, pieces, sems, 3)
    copies += load([(offset, out)], sems, 2)
    finish(copies)


def slab_offset(place, images, field, low, high, kernels, decay, matrix, group, chunks):
    layers, taps, channels = kernels.shape
    shape = images.shape
    count = group * len(chunks)
    results = pl.pallas_call(
        functools.partial(offset_kernel, layers, group, chunks),
        out_shape=[jax.ShapeDtypeStruct(shape, F32)] + piece_shapes(shape, group, chunks),
        in_specs=[SMEM, ANY, VMEM, VMEM, VMEM, ANY, VMEM, VMEM],
        out_specs=[ANY] * (1 + count),
        scratch_shapes=[pltpu.VMEM(shape, F32), pltpu.VMEM(kernels.shape, BF16)]
        + [pltpu.VMEM(shape, F32)] * 2
        + scratch_of(shape, 2)
        + [pltpu.VMEM((taps, channels), BF16), pltpu.SemaphoreType.DMA((3 + count,))],
        compiler_params=params(),
        cost_estimate=cost(shape, layers + 1),
    )(place, images, field, low, high, kernels, decay, matrix)
    return results[0], results[1:]


def split_matrix(matrix):
    high = matrix.astype(BF16)
    low = (matrix - high.astype(F32)).astype(BF16)
    return jnp.concatenate([high, high, low], axis=0)


def split_rows(rows):
    high = rows.astype(BF16)
    low = (rows - high.astype(F32)).astype(BF16)
    return jnp.concatenate([high, low, high], axis=1)


def identity(channels):
    rows = lax.broadcasted_iota(jnp.int32, (channels, channels), 0)
    columns = lax.broadcasted_iota(jnp.int32, (channels, channels), 1)
    return (rows == columns).astype(F32)


def prelude_kernel(place, kernels, damping, *outs):
    layers, taps, channels = kernels.shape
    parts, (quarter, matrix, turned) = outs[:layers], outs[layers:]
    half_rows, quarter_rows = taps // 2, taps // 4
    half, chunk = lax.rem(place[CHUNK], 2), lax.rem(place[CHUNK], 4)
    for layer in range(layers):
        rate = jnp.broadcast_to(damping[layer : layer + 1], (8, channels))
        parts[layer][0:half_rows] = kernels[layer, pl.ds(half * half_rows, half_rows)].astype(F32)
        parts[layer][half_rows : half_rows + 8] = rate
        quarter[layer, 0:quarter_rows] = kernels[layer, pl.ds(chunk * quarter_rows, quarter_rows)].astype(F32)
        quarter[layer, quarter_rows : quarter_rows + 8] = rate
    total = kernels[0, 0:channels].astype(F32)
    for tap in range(1, taps // channels):
        total += kernels[0, tap * channels : (tap + 1) * channels].astype(F32)
    diagonal = identity(channels) * (1.0 - layers * STEP * damping[0:1])
    coarse = diagonal + layers * STEP * total
    matrix[...] = coarse
    turned[...] = coarse.T


def prelude(place, kernels, damping):
    layers, taps, channels = kernels.shape
    part = jax.ShapeDtypeStruct((taps // 2 + 8, channels), F32)
    quarter = jax.ShapeDtypeStruct((layers, taps // 4 + 8, channels), F32)
    square = jax.ShapeDtypeStruct((channels, channels), F32)
    results = pl.pallas_call(
        prelude_kernel,
        out_shape=[part] * layers + [quarter, square, square],
        in_specs=[SMEM] + [VMEM] * 2,
        out_specs=[VMEM] * (layers + 3),
        compiler_params=params(16),
    )(place, kernels, damping)
    return results[:layers], *results[layers:]


def step_at(group, index):
    return index


def before_at(group, index):
    return group + index


def after_at(group, index):
    return 2 * group + index


def whole_at(group):
    return 3 * group


def matrices_kernel(group, place, *refs):
    pieces, (out, held) = refs[:group], refs[group:]
    channels = held.shape[1]
    for shift in range(group):
        held[lax.rem(place[FORWARD] - shift + group, group)] = pieces[shift][...]
    for backward in range(2):
        ordered = [held[group - 1 - step].T if backward else held[step] for step in range(group)]
        product = identity(channels)
        for step in range(group):
            split = split_matrix(ordered[step])
            out[backward, step_at(group, step)] = split
            out[backward, before_at(group, step)] = split_matrix(product)
            product = ordered[0] if step == 0 else jnp.dot(split_rows(product), split, preferred_element_type=F32)
        out[backward, whole_at(group)] = split_matrix(product)
        product = identity(channels)
        for step in reversed(range(group)):
            out[backward, after_at(group, step)] = split_matrix(product)
            if step == group - 1:
                product = ordered[step]
            else:
                product = jnp.dot(split_rows(ordered[step]), split_matrix(product), preferred_element_type=F32)


def group_matrices(place, pieces):
    group = len(pieces)
    channels = pieces[0].shape[0]
    return pl.pallas_call(
        functools.partial(matrices_kernel, group),
        out_shape=jax.ShapeDtypeStruct((2, 3 * group + 1, 3 * channels, channels), BF16),
        in_specs=[SMEM] + [VMEM] * group,
        out_specs=VMEM,
        scratch_shapes=[pltpu.VMEM((group, channels, channels), F32)],
        compiler_params=params(16),
    )(place, *pieces)


def flat_of(shape):
    return (shape[0] * shape[1] * shape[2], shape[3])


def carry_kernel(group, chunks, chunk, backward, place, seed, matrices, *refs):
    pieces, (carry, start, right, sems) = refs[:group], refs[group:]
    member = place[BACKWARD if backward else FORWARD]
    leads = place[BACKWARD_HEAD if backward else FORWARD_HEAD] == 1
    depth = right.shape[0] // (group + 1)
    source = piece_refs(member, group, chunks, seed, 0, chunk, True)
    loads = [(source, start), (matrices.at[backward, whole_at(group)], right.at[pl.ds(group * depth, depth)])]
    for shift in range(group):
        slab = lax.rem(member - shift + group, group)
        loads.append((matrices.at[backward, after_at(group, slab)], right.at[pl.ds(shift * depth, depth)]))
    loads = load(loads, sems, 0)
    flat = flat_of(start.shape)
    left = [split_rows(pieces[shift][...].reshape(flat)) for shift in range(group)]
    finish(loads)
    left.append(split_rows(jnp.where(leads, start[...], 0.0).reshape(flat)))
    total = jnp.dot(jnp.concatenate(left, axis=1), right[...], preferred_element_type=F32)
    carry[...] = total.reshape(start.shape)


def group_carry(place, seed, matrices, pieces, group, chunks, chunk, backward):
    shape = pieces[0].shape
    depth, channels = matrices.shape[2:]
    return pl.pallas_call(
        functools.partial(carry_kernel, group, chunks, chunk, int(backward)),
        out_shape=jax.ShapeDtypeStruct(shape, F32),
        in_specs=[SMEM, ANY, ANY] + [VMEM] * group,
        out_specs=VMEM,
        scratch_shapes=[
            pltpu.VMEM(shape, F32),
            pltpu.VMEM(((group + 1) * depth, channels), BF16),
            pltpu.SemaphoreType.DMA((group + 2,)),
        ],
        compiler_params=params(24),
        cost_estimate=small_cost(shape, 5),
    )(place, seed, matrices, *pieces)


def partial_kernel(group, chunks, chunk, backward, place, seed, matrices, *refs):
    pieces, (begun, products, full, held, start, sets, sems) = refs[:group], refs[group:]
    member = place[BACKWARD if backward else FORWARD]
    leads = place[BACKWARD_HEAD if backward else FORWARD_HEAD] == 1
    source = piece_refs(member, group, chunks, seed, 0, chunk, True)
    loads = load([(source, start), (matrices.at[backward, pl.ds(0, 2 * group)], sets)], sems, 0)
    for shift in range(group):
        held[lax.rem(member - shift + group, group)] = pieces[shift][...]
    finish(loads)
    shape = start.shape
    flat = flat_of(shape)
    state = jnp.where(leads, start[...], 0.0).reshape(flat)
    full[0] = state.reshape(shape)
    for slab in range(group - 1):
        step = sets[step_at(group, slab)]
        state = jnp.dot(split_rows(state), step, preferred_element_type=F32) + held[slab].reshape(flat)
        full[slab + 1] = state.reshape(shape)
    channels = shape[3]
    for shift in range(group):
        slab = lax.rem(member + shift, group)
        begun[shift] = full[slab]
        products[:, shift * channels : (shift + 1) * channels] = sets[before_at(group, slab)]


def partial_chain(place, seed, matrices, pieces, group, chunks, chunk, backward):
    shape = pieces[0].shape
    depth, channels = matrices.shape[2:]
    stack = (group,) + shape
    return pl.pallas_call(
        functools.partial(partial_kernel, group, chunks, chunk, int(backward)),
        out_shape=[jax.ShapeDtypeStruct(stack, F32), jax.ShapeDtypeStruct((depth, group * channels), BF16)],
        in_specs=[SMEM, ANY, ANY] + [VMEM] * group,
        out_specs=[VMEM] * 2,
        scratch_shapes=[
            pltpu.VMEM(stack, F32),
            pltpu.VMEM(stack, F32),
            pltpu.VMEM(shape, F32),
            pltpu.VMEM((2 * group, depth, channels), BF16),
            pltpu.SemaphoreType.DMA((2,)),
        ],
        compiler_params=params(24),
        cost_estimate=small_cost(shape, 12),
    )(place, seed, matrices, *pieces)


def hop_kernel(carry, whole, own, result):
    shape = own.shape
    moved = jnp.dot(split_rows(carry[...].reshape(flat_of(shape))), whole[...], preferred_element_type=F32)
    result[...] = own[...] + moved.reshape(shape)


def hop(carry, whole, own):
    return pl.pallas_call(
        hop_kernel,
        out_shape=jax.ShapeDtypeStruct(own.shape, F32),
        in_specs=[VMEM] * 3,
        out_specs=VMEM,
        compiler_params=params(24),
        cost_estimate=small_cost(own.shape, 2),
    )(carry, whole, own)


def complete_kernel(group, carry, products, begun, *outs):
    shape = carry.shape
    channels = shape[3]
    moved = jnp.dot(split_rows(carry[...].reshape(flat_of(shape))), products[...], preferred_element_type=F32)
    for shift in range(group):
        part = moved[:, shift * channels : (shift + 1) * channels]
        outs[shift][...] = begun[shift] + part.reshape(shape)


def complete_chain(carry, products, begun, group):
    shape = carry.shape
    return pl.pallas_call(
        functools.partial(complete_kernel, group),
        out_shape=[jax.ShapeDtypeStruct(shape, F32)] * group,
        in_specs=[VMEM] * 3,
        out_specs=[VMEM] * group,
        compiler_params=params(24),
        cost_estimate=small_cost(shape, 4),
    )(carry, products, begun)


def middle_kernel(layers, group, chunks, place, *refs):
    count_pieces = group * len(chunks)
    pieces, refs = refs[:count_pieces], refs[count_pieces:]
    (offset_hbm, cotangent_hbm, next_k_hbm, next_f_hbm, own_k_hbm, own_f_hbm, own_decay, next_decay, matrix, turned) = refs[:10]
    refs = refs[10:]
    (slab_end, coarse_end, back_offset), refs = refs[:3], refs[3:]
    state_outs, refs = refs[:layers], refs[layers:]
    act_outs, refs = refs[:layers], refs[layers:]
    back_pieces, refs = refs[:count_pieces], refs[count_pieces:]
    (begins, states, acts, offset, cotangent, tops, adjoint, first_columns, second_columns, paired) = refs[:10]
    kernels, turned_kernels, decays, sems = refs[10:]
    pairs = offset.shape[0]
    last_slab = place[POSITION] == place[SIZE] - 1

    brought = bring_in(place[FORWARD], group, chunks, pieces, begins, sems, 0)
    base = count_pieces
    loads = load(
        [
            (offset_hbm, offset),
            (next_k_hbm, kernels.at[0]),
            (cotangent_hbm, tops),
            (next_f_hbm, turned_kernels.at[0]),
            (own_k_hbm, kernels.at[1]),
            (own_f_hbm, turned_kernels.at[1]),
            (cotangent_hbm, cotangent),
        ],
        sems,
        base,
    )
    base += len(loads)
    decays[0] = next_decay[...]
    decays[1] = own_decay[...]
    clear_borders(first_columns)
    clear_borders(second_columns)
    finish(brought)
    loads[0].wait()

    def coarse_rows(first, count):
        rows = pl.ds(first, count)
        for odd in range(2):
            fresh = transform_rows(begins[rows, odd], matrix[...]) + offset[rows, odd]
            states[0, rows, odd] = fresh
            put_columns(first_columns, first, odd, fresh)

    per_block(pairs, coarse_rows)
    out_coarse = pltpu.make_async_copy(states.at[0], coarse_end, sems.at[base])
    out_coarse.start()
    base += 1
    finish(loads[1:])
    late = [(states.at[layers], slab_end)]
    late += [(states.at[n], state_outs[n]) for n in range(layers)]
    late += [(acts.at[n], act_outs[n]) for n in range(layers)]

    def both_sweeps(index, carry):
        now, later = first_columns, second_columns
        for layer in range(layers):
            spread(paired, kernels[index, layer])

            def store(rows, first, odd, following, activation, layer=layer, target=later):
                states[layer + 1, rows, odd] = following
                acts[layer, rows, odd] = activation
                if layer < layers - 1:
                    put_columns(target, first, odd, following)
                else:
                    put_columns(target, first, odd, scaled_rows(tops[rows, odd], activation))

            forward_layer(states.at[layer], now, paired, decays[index, layer : layer + 1], store)
            now, later = later, now

        @pl.when(index == 1)
        def _():
            load(late, sems, base)

        for layer in reversed(range(layers)):
            spread(paired, turned_kernels[index, layer])

            def store_back(rows, first, odd, following, layer=layer, target=later):
                adjoint[rows, odd] = following
                if layer > 0:
                    put_columns(target, first, odd, scaled_rows(following, acts[layer - 1, rows, odd]))

            source = tops if layer == layers - 1 else adjoint
            backward_layer(source, now, paired, decays[index, layer : layer + 1], store_back)
            now, later = later, now

        @pl.when(index == 0)
        def _():
            out_coarse.wait()

            def again(first, count):
                rows = pl.ds(first, count)
                tops[rows] = jnp.where(last_slab, cotangent[rows], adjoint[rows])
                for odd in range(2):
                    begin = begins[rows, odd]
                    states[0, rows, odd] = begin
                    put_columns(first_columns, first, odd, begin)

            per_block(pairs, again)

        return carry

    lax.fori_loop(0, 2, both_sweeps, 0)

    def subtract(first, count):
        rows = pl.ds(first, count)
        for odd in range(2):
            adjoint[rows, odd] = adjoint[rows, odd] - transform_rows(tops[rows, odd], turned[...])

    per_block(pairs, subtract)
    outs = send_out(place[BACKWARD], group, chunks, adjoint, back_pieces, sems, 0)
    outs += load([(adjoint, back_offset)], sems, count_pieces)
    finish(outs)
    for number, (source, target) in enumerate(late):
        pltpu.make_async_copy(source, target, sems.at[base + number]).wait()


def middle(place, pieces, offset, cotangent, own, following, own_decay, next_decay, matrix, turned, group, chunks):
    layers = own[0].shape[0]
    field = offset.shape
    count = len(pieces)
    fields = [jax.ShapeDtypeStruct(field, F32)] * (3 + 2 * layers)
    results = pl.pallas_call(
        functools.partial(middle_kernel, layers, group, chunks),
        out_shape=fields + piece_shapes(field, group, chunks),
        in_specs=[SMEM] + [ANY] * (count + 6) + [VMEM] * 4,
        out_specs=[ANY] * (3 + 2 * layers + count),
        scratch_shapes=[pltpu.VMEM(field, F32)]
        + [pltpu.VMEM((layers + 1,) + field, F32), pltpu.VMEM((layers,) + field, F32)]
        + [pltpu.VMEM(field, F32)] * 4
        + scratch_of(field, 2)
        + [pltpu.VMEM((2,) + own[0].shape, BF16)] * 2
        + [pltpu.VMEM((2, layers, field[3]), F32), pltpu.SemaphoreType.DMA((count + 9 + 2 * layers,))],
        compiler_params=params(52),
        cost_estimate=cost(field, 4 * layers),
    )(place, *pieces, offset, cotangent, *following, *own, own_decay, next_decay, matrix, turned)
    return results[:3], results[3 : 3 + layers], results[3 + layers : 3 + 2 * layers], results[3 + 2 * layers :]


def turn(whole, turned):
    taps, channels = whole.shape[0] // whole.shape[1], whole.shape[1]
    for tap in range(taps):
        block = whole[tap * channels : (tap + 1) * channels]
        other = taps - 1 - tap
        turned[other * channels : (other + 1) * channels] = block.T.astype(BF16)


def own_kernel(kernels, turned, whole):
    for layer in range(kernels.shape[0]):
        whole[...] = kernels[layer].astype(F32)
        turn(whole, turned.at[layer])


def turn_own(kernels):
    return pl.pallas_call(
        own_kernel,
        out_shape=jax.ShapeDtypeStruct(kernels.shape, BF16),
        in_specs=[VMEM],
        out_specs=VMEM,
        scratch_shapes=[pltpu.VMEM(kernels.shape[1:], F32)],
        compiler_params=params(),
    )(kernels)


def next_kernel(place, *refs):
    quarters, (kernels, turned, decay, whole) = refs[:4], refs[4:]
    layers = kernels.shape[0]
    rows = whole.shape[0] // 4
    chunk = lax.rem(place[CHUNK], 4)
    at = [chunk, chunk + 2 - 4 * (chunk // 2), chunk + 1 - 2 * lax.rem(chunk, 2)]
    at.append(at[2] + 2 - 4 * (chunk // 2))
    for layer in range(layers):
        for number in range(4):
            whole[pl.ds(at[number] * rows, rows)] = quarters[number][layer, 0:rows]
        kernels[layer] = whole[...].astype(BF16)
        turn(whole, turned.at[layer])
        decay[layer : layer + 1] = quarters[0][layer, rows : rows + 1]


def join_next(place, quarters):
    layers, rows, channels = quarters[0].shape
    shape = (layers, 4 * (rows - 8), channels)
    results = pl.pallas_call(
        next_kernel,
        out_shape=[jax.ShapeDtypeStruct(shape, BF16)] * 2 + [jax.ShapeDtypeStruct((layers, channels), F32)],
        in_specs=[SMEM] + [VMEM] * 4,
        out_specs=[VMEM] * 3,
        scratch_shapes=[pltpu.VMEM(shape[1:], F32)],
        compiler_params=params(),
    )(place, *quarters)
    return results[:2], results[2]


def turned_columns_kernel(state, turned, columns):
    pairs, _, side, _ = state.shape
    wide, depth = columns.shape[2:]
    clear_borders(columns)

    def fill(first, count):
        for odd in range(2):
            put_columns(columns, first, odd, state[pl.ds(first, count), odd])

    per_block(pairs, fill)
    for pair in range(pairs + 1):
        block = columns[pair].reshape(2 * wide, depth).astype(F32)
        turned[:, pair * 2 * wide : (pair + 1) * 2 * wide] = block.T.astype(BF16)


def turned_columns(state):
    shape = columns_shape(state.shape)
    return pl.pallas_call(
        turned_columns_kernel,
        out_shape=jax.ShapeDtypeStruct((shape[3], shape[0] * 2 * shape[2]), BF16),
        in_specs=[VMEM],
        out_specs=VMEM,
        scratch_shapes=[pltpu.VMEM(shape, BF16)],
        compiler_params=params(),
        cost_estimate=cost(state.shape, 1),
    )(state)


def gradient_body(adjoint, activation, turned, ready, shifted, gradient, side):
    pairs = adjoint.shape[0]
    wide = shifted.shape[2]
    channels = adjoint.shape[3]
    edge = jnp.zeros((wide, channels), BF16)
    flat = 2 * pairs + 2
    for tap in range(3):
        for row in list(range(tap)) + list(range(flat - 2 + tap, flat)):
            shifted[row // 2, row % 2, :, tap * channels : (tap + 1) * channels] = edge

    def fill(first, count):
        rows = pl.ds(first, count)
        for odd in range(2):
            scaled = scaled_rows(adjoint[rows, odd], activation[rows, odd])
            padded = jnp.concatenate([scaled, jnp.zeros((count, wide - side, channels), F32)], axis=1).astype(BF16)
            for tap in range(3):
                row = odd + tap
                shifted[pl.ds(first + row // 2, count), row % 2, :, tap * channels : (tap + 1) * channels] = padded

    per_block(pairs, fill)
    ready()
    products = jnp.dot(
        turned[...], shifted[...].reshape(flat * wide, 3 * channels), preferred_element_type=F32
    )
    for row in range(3):
        for column in range(3):
            tap = 3 * row + column
            gradient[tap * channels : (tap + 1) * channels] = products[
                column * channels : (column + 1) * channels, row * channels : (row + 1) * channels
            ]


def halve(place, gradient, keep, send):
    half = lax.rem(place[CHUNK], 2)
    rows = keep.shape[0]
    keep[...] = gradient[pl.ds(half * rows, rows)]
    send[...] = gradient[pl.ds((1 - half) * rows, rows)]


def top_kernel(group, chunks, place, *refs):
    count_pieces = group * len(chunks)
    pieces, refs = refs[:count_pieces], refs[count_pieces:]
    activation_hbm, turned_hbm, adjoint_out, keep, send = refs[:5]
    adjoint, activation, turned, shifted, gradient, sems = refs[5:]
    brought = bring_in(place[BACKWARD], group, chunks, pieces, adjoint, sems, 0)
    loads = load([(activation_hbm, activation), (turned_hbm, turned)], sems, count_pieces)
    finish(brought)
    out = load([(adjoint, adjoint_out)], sems, 0)
    loads[0].wait()
    gradient_body(adjoint, activation, turned, loads[1].wait, shifted, gradient, adjoint.shape[2])
    halve(place, gradient, keep, send)
    finish(out)


def top_gradient(place, pieces, activation, turned, group, chunks):
    field = activation.shape
    shape = columns_shape(field)
    taps = 9 * field[3]
    half = jax.ShapeDtypeStruct((taps // 2, field[3]), F32)
    return pl.pallas_call(
        functools.partial(top_kernel, group, chunks),
        out_shape=[jax.ShapeDtypeStruct(field, F32), half, half],
        in_specs=[SMEM] + [ANY] * (len(pieces) + 2),
        out_specs=[ANY, VMEM, VMEM],
        scratch_shapes=[
            pltpu.VMEM(field, F32),
            pltpu.VMEM(field, F32),
            pltpu.VMEM(turned.shape, BF16),
            pltpu.VMEM(shape, BF16),
            pltpu.VMEM((taps, field[3]), F32),
            pltpu.SemaphoreType.DMA((len(pieces) + 2,)),
        ],
        compiler_params=params(),
        cost_estimate=cost(field, 1),
    )(place, *pieces, activation, turned)


def retreat_body(adjoint, activation, columns, paired, rate, store):
    clear_borders(columns)
    fill_backward(adjoint, activation, columns)
    backward_layer(adjoint, columns, paired, rate, store)


def lower_kernel(layer, place, adjoint, above, kernel, decay, below_hbm, turned_hbm, *refs):
    result_out, keep, send = refs[:3]
    result, below, turned, columns, paired, shifted, gradient, sems = refs[3:]
    loads = load([(below_hbm, below), (turned_hbm, turned)], sems, 0)
    spread(paired, kernel[layer])

    def store(rows, first, odd, fresh):
        result[rows, odd] = fresh

    retreat_body(adjoint, above, columns, paired, decay[layer : layer + 1], store)
    out = load([(result, result_out)], sems, 2)
    loads[0].wait()
    gradient_body(result, below, turned, loads[1].wait, shifted, gradient, result.shape[2])
    halve(place, gradient, keep, send)
    finish(out)


def lower_gradient(place, layer, adjoint, above, kernels, decay, below, turned):
    field = adjoint.shape
    shape = columns_shape(field)
    taps = 9 * field[3]
    half = jax.ShapeDtypeStruct((taps // 2, field[3]), F32)
    return pl.pallas_call(
        functools.partial(lower_kernel, layer),
        out_shape=[jax.ShapeDtypeStruct(field, F32), half, half],
        in_specs=[SMEM] + [VMEM] * 4 + [ANY] * 2,
        out_specs=[ANY, VMEM, VMEM],
        scratch_shapes=[pltpu.VMEM(field, F32), pltpu.VMEM(field, F32), pltpu.VMEM(turned.shape, BF16)]
        + scratch_of(field, 1)
        + [pltpu.VMEM(shape, BF16), pltpu.VMEM((taps, field[3]), F32), pltpu.SemaphoreType.DMA((3,))],
        compiler_params=params(),
        cost_estimate=cost(field, 2),
    )(place, adjoint, above, kernels, decay, below, turned)


def last_kernel(adjoint, activation, kernel, decay, tops, back_offset, turned, result, adjoint_end, columns, paired):
    spread(paired, kernel[0])

    def store(rows, first, odd, fresh):
        result[rows, odd] = fresh

    retreat_body(adjoint, activation, columns, paired, decay[0:1], store)

    def coarse_rows(first, count):
        rows = pl.ds(first, count)
        for odd in range(2):
            adjoint_end[rows, odd] = transform_rows(tops[rows, odd], turned[...]) + back_offset[rows, odd]

    per_block(adjoint.shape[0], coarse_rows)


def last_retreat(adjoint, activation, kernels, decay, tops, back_offset, turned):
    field = adjoint.shape
    return pl.pallas_call(
        last_kernel,
        out_shape=[jax.ShapeDtypeStruct(field, F32)] * 2,
        in_specs=[VMEM] * 7,
        out_specs=[VMEM] * 2,
        scratch_shapes=scratch_of(field, 1),
        compiler_params=params(),
        cost_estimate=cost(field, 1),
    )(adjoint, activation, kernels, decay, tops, back_offset, turned)


def collect_kernel(layers, place, *refs):
    sources, out = refs[: 2 * layers], refs[2 * layers]
    half = lax.rem(place[CHUNK], 2)
    rows = out.shape[1] // 2
    for layer in range(layers):
        out[layer, pl.ds(half * rows, rows)] = sources[2 * layer][...]
        out[layer, pl.ds((1 - half) * rows, rows)] = sources[2 * layer + 1][...]


def collect(place, halves):
    layers = len(halves)
    rows, channels = halves[0][0].shape
    flat = [half for both in halves for half in both]
    return pl.pallas_call(
        functools.partial(collect_kernel, layers),
        out_shape=jax.ShapeDtypeStruct((layers, 2 * rows, channels), F32),
        in_specs=[SMEM] + [VMEM] * (2 * layers),
        out_specs=VMEM,
        compiler_params=params(16),
    )(place, *flat)


def from_behind(shard, axis, by):
    devices = lax.axis_size(axis)
    pairs = [(i, i + by) for i in range(devices) if 0 <= i + by < devices]
    return lax.ppermute(shard, axis, pairs)


def swap(shard, bit):
    return lax.ppermute(shard, "dp", [(i, i ^ bit) for i in range(lax.axis_size("dp"))])


def order_of(index, size, backward):
    return size - 1 - index if backward else index


def group_of(size):
    for group in (GROUP, 2, 1):
        if size % group == 0:
            return group


def exchange(pieces, group, backward):
    size = lax.axis_size("layer")
    received = [pieces[0]]
    for shift in range(1, group):
        pairs = []
        for order in range(size):
            base = order - order % group
            target = base + (order + shift) % group
            pairs.append((order_of(order, size, backward), order_of(target, size, backward)))
        received.append(lax.ppermute(pieces[shift], "layer", pairs))
    return received


def coarse_chain(place, seed, pieces, matrices, group, chunks, backward):
    size = lax.axis_size("layer")
    pairs = [(order_of(i, size, backward), order_of(i + group, size, backward)) for i in range(size - group)]
    received = [exchange(pieces[c * group : (c + 1) * group], group, backward) for c in range(len(chunks))]
    begins = []
    for chunk in range(len(chunks)):
        carry = jnp.zeros(pieces[chunk * group].shape, F32)
        if size > group:
            out = group_carry(place, seed, matrices, received[chunk], group, chunks, chunk, backward)
            carry = lax.ppermute(out, "layer", pairs)
            for _ in range(size // group - 2):
                carry = lax.ppermute(hop(carry, matrices[int(backward), whole_at(group)], out), "layer", pairs)
        begun, products = partial_chain(place, seed, matrices, received[chunk], group, chunks, chunk, backward)
        begins.append((carry, products, begun))
    result = []
    for carry, products, begun in begins:
        result += exchange(complete_chain(carry, products, begun, group), group, backward)
    return result


def sum_across(total):
    bit = 2
    while bit < lax.axis_size("dp"):
        total = total + swap(total, bit)
        bit *= 2
    return total


def per_device(images, kernels, damping, cotangent):
    layers, taps, channels = kernels.shape
    _, height, side, _ = images.shape
    size = lax.axis_size("layer")
    position = lax.axis_index("layer")
    dp_at = lax.axis_index("dp")
    field = (height // 2, 2, side, channels)
    images = images.reshape(field)
    cotangent = cotangent.reshape(field)
    group = group_of(size)
    quarter = field[0] // group
    chunks = chunks_of(quarter)
    back_order = size - 1 - position
    place = jnp.stack(
        [
            position,
            lax.rem(position, group),
            lax.rem(back_order, group),
            dp_at,
            (position < group).astype(jnp.int32),
            (back_order < group).astype(jnp.int32),
            jnp.int32(size),
            jnp.int32(0),
        ]
    ).astype(jnp.int32)

    parts, quarter_part, matrix, turned_matrix = prelude(place, kernels, damping)

    lows = [from_behind(part, "layer", 1) for part in parts]
    highs = [swap(low, 1) for low in lows]

    matrices = group_matrices(place, exchange([matrix] * group, group, False))
    own = (kernels, turn_own(kernels))

    state, matrices = lax.optimization_barrier((images, matrices))
    for layer in range(layers - 1):
        state = fetched_layer(place, state, lows[layer], highs[layer])

    quarter_part, state = lax.optimization_barrier((quarter_part, state))
    first = from_behind(quarter_part, "layer", -1)
    second = swap(first, 2)
    following, next_decay = join_next(place, [first, second, swap(first, 1), swap(second, 1)])

    offset, pieces = slab_offset(
        place, images, state, lows[-1], highs[-1], kernels, damping, matrix, group, chunks
    )
    pieces = coarse_chain(place, images, pieces, matrices, group, chunks, False)
    (slab_end, coarse_end, back_offset), states, acts, pieces = middle(
        place, pieces, offset, cotangent, own, following, damping, next_decay, matrix, turned_matrix, group, chunks
    )
    turned = [turned_columns(state) for state in states]
    pieces = coarse_chain(place, cotangent, pieces, matrices, group, chunks, True)
    tops, keep, send = top_gradient(place, pieces, acts[-1], turned[-1], group, chunks)
    adjoint = tops
    paired = [None] * layers
    halves = [None] * layers
    for layer in reversed(range(1, layers)):
        paired[layer] = (keep, send)
        adjoint, keep, send = lower_gradient(
            place, layer, adjoint, acts[layer], own[1], damping, acts[layer - 1], turned[layer - 1]
        )
        total = paired[layer][0] + swap(paired[layer][1], 1)
        adjoint, total = lax.optimization_barrier((adjoint, total))
        if layer < layers - 1:
            adjoint, summed = lax.optimization_barrier((adjoint, paired[layer + 1]))
            paired[layer + 1] = summed
        paired[layer] = sum_across(total)
    total = keep + swap(send, 1)
    adjoint, adjoint_end = last_retreat(adjoint, acts[0], own[1], damping, tops, back_offset, turned_matrix)
    adjoint, total, paired[1] = lax.optimization_barrier((adjoint, total, paired[1]))
    paired[0] = sum_across(total)
    halves = [(half, swap(half, 1)) for half in paired]
    full = (1, 1, height, side, channels)
    return (
        slab_end.reshape(full),
        coarse_end.reshape(full),
        adjoint.reshape(full),
        adjoint_end.reshape(full),
        collect(place, halves),
    )


def solution(mesh):
    in_specs = (
        P("dp", None, None, None),
        P("layer", None, None),
        P("layer", None),
        P("dp", None, None, None),
    )
    out_specs = (
        P("layer", "dp", None, None, None),
        P("layer", "dp", None, None, None),
        P("layer", "dp", None, None, None),
        P("layer", "dp", None, None, None),
        P("layer", None, None),
    )
    return jax.shard_map(
        per_device, mesh=mesh, in_specs=in_specs, out_specs=out_specs, check_vma=False
    )
```

time: 810 us -> 271 us (0.33); the launches traced: 796 us -> 271 us
  waiting for transfers between devices: 266 us -> 113 us
  matrix products: 146 us -> 0 us
  local copies, waits for them, and re-layouts: 150 us -> 6.06 us
  starting transfers between devices: 158 us -> 58.8 us
  Pallas kernels: 0 us -> 91.9 us
  other arithmetic: 58.8 us -> 0.2 us
  between operations: 16 us -> 1.14 us
    ppermute x48 -> x4, waiting for transfers between devices: 227 us -> 10.2 us  [from_behind(): return lax.ppermute(shard, axis, pairs)]
    dot_general x71 -> x0, matrix products: 146 us -> none  [the longest x50 86.2 us: high_dot(): jnp.dot(left, right, precision=lax.Precision.HIGHEST, preferred_element_t...]
    ppermute x48 -> x4, starting transfers between devices: 158 us -> 13.1 us  [from_behind(): return lax.ppermute(shard, axis, pairs)]
    ppermute x0 -> x32, waiting for transfers between devices: none -> 103 us  [the longest x15 62 us: exchange(): received.append(lax.ppermute(pieces[shift], 'layer', pairs))]
    pallas_call x0 -> x22, Pallas kernels: none -> 91.9 us  [the longest x1 33.7 us: middle(): pl.pallas_call(functools.partial(middle_kernel, layers, group, chunks), o...]
    unnamed x227 -> x44, local copies, waits for them, and re-layouts: 77.4 us -> 5.97 us
    dynamic_update_slice x46 -> x0, local copies, waits for them, and re-layouts: 54.4 us -> none  [advance_block(): lax.dynamic_update_slice_in_dim(collected, jnp.where(inside, entering, ol...]
    ppermute x0 -> x32, starting transfers between devices: none -> 45.7 us  [the longest x15 33.9 us: exchange(): received.append(lax.ppermute(pieces[shift], 'layer', pairs))]
  transfers between devices with their start and end apart: 49 -> 36, of which waited for: 49 -> 23; matrix products, arithmetic and copies ran while one was open for 5% -> 0% of each run, Pallas kernels for 0% -> 18%
where the time goes in v1:
time: 271 us
  waiting for transfers between devices  113 us (42%)
  Pallas kernels  91.9 us (34%)
  starting transfers between devices  58.8 us (22%)
  local copies, waits for them, and re-layouts  6.06 us (2%)
    ppermute x15, waiting for transfers between devices, exchange(): received.append(lax.ppermute(pieces[shift], 'layer', pairs))  62 us
    ppermute x15, starting transfers between devices, exchange(): received.append(lax.ppermute(pieces[shift], 'layer', pairs))  33.9 us
    pallas_call x1, Pallas kernels, middle(): pl.pallas_call(functools.partial(middle_kernel, layers, group, chunks), o...  33.7 us
    ppermute x2, waiting for transfers between devices, coarse_chain(): carry = lax.ppermute(out, 'layer', pairs)  24.2 us
    ppermute x15, waiting for transfers between devices, swap(): lax.ppermute(shard, 'dp', [(i, i ^ bit) for i in range(lax.axis_size('dp'...  16.5 us
    ppermute x4, starting transfers between devices, from_behind(): return lax.ppermute(shard, axis, pairs)  13.1 us
    pallas_call x2, Pallas kernels, lower_gradient(): pl.pallas_call(functools.partial(lower_kernel, layer), out_shape=[jax.Sha...  11.9 us
    pallas_call x1, Pallas kernels, slab_offset(): pl.pallas_call(functools.partial(offset_kernel, layers, group, chunks), o...  11.3 us
  transfers between devices with their start and end apart: 36, of which 23 were waited for; matrix products, arithmetic and copies ran while one was open for 0% of the time, Pallas kernels for 18%

profile of v1, /device:TPU:0, one launch (start us, length us, event | category | flops | bytes accessed | tf_op | source)
XLA Modules:
  0.0 271.0 jit_solution(8305297282520761312)
XLA Ops:
  3.3 5.0 %collective-permute-start.3 = (f32[584,128]{1,0:T(8,128)S(1)}, f32[584,128]{1,0:T(8,128)S(1)}, u32[]{:S(2)}, u32[]{:S(2)}) collective-permute-start(f32[584,128]{1,0:T(8,128)S(1)} %get-tuple-element.72), channel_id=1, source_target_pairs={{0,4},{4,8},{8,12},{12,16},{16,20},{20,24},{24,28},{1,5},{5,9},{9,... | collective-permute-start | bytes 897032 | tf_op jit(solution)/shard_map/ppermute | solution.py:938
  8.3 3.5 %collective-permute-start.5 = (f32[584,128]{1,0:T(8,128)S(1)}, f32[584,128]{1,0:T(8,128)S(1)}, u32[]{:S(2)}, u32[]{:S(2)}) collective-permute-start(f32[584,128]{1,0:T(8,128)S(1)} %get-tuple-element.73), channel_id=1, source_target_pairs={{0,4},{4,8},{8,12},{12,16},{16,20},{20,24},{24,28},{1,5},{5,9},{9,... | collective-permute-start | bytes 897032 | tf_op jit(solution)/shard_map/ppermute | solution.py:938
  11.8 3.4 %collective-permute-start.7 = (f32[584,128]{1,0:T(8,128)S(1)}, f32[584,128]{1,0:T(8,128)S(1)}, u32[]{:S(2)}, u32[]{:S(2)}) collective-permute-start(f32[584,128]{1,0:T(8,128)S(1)} %get-tuple-element.75), channel_id=1, source_target_pairs={{0,4},{4,8},{8,12},{12,16},{16,20},{20,24},{24,28},{1,5},{5,9},{9,... | collective-permute-start | bytes 897032 | tf_op jit(solution)/shard_map/ppermute | solution.py:938
  15.8 6.4 %collective-permute-done.5.low = f32[584,128]{1,0:T(8,128)S(1)} collective-permute-done((f32[584,128]{1,0:T(8,128)S(1)}, f32[584,128]{1,0:T(8,128)S(1)}, u32[]{:S(2)}, u32[]{:S(2)}) %collective-permute-start.5) | collective-permute-done | bytes 299040 | tf_op jit(solution)/shard_map/ppermute | solution.py:938
  22.2 3.5 %collective-permute-start.2 = (f32[128,128]{1,0:T(8,128)S(1)}, f32[128,128]{1,0:T(8,128)S(1)}, u32[]{:S(2)}, u32[]{:S(2)}) collective-permute-start(f32[128,128]{1,0:T(8,128)S(1)} %get-tuple-element.68.refs_0_.matrix.refs_12_), channel_id=1, source_target_pairs={{0,12},{4,0},{8,4},{12,8},{16,28},{20,16},{24,20},{28,24},{1,13},{... | collective-permute-start | bytes 196616 | tf_op jit(solution)/shard_map/ppermute | solution.py:964
  25.7 3.2 %collective-permute-done.7.low = f32[584,128]{1,0:T(8,128)S(1)} collective-permute-done((f32[584,128]{1,0:T(8,128)S(1)}, f32[584,128]{1,0:T(8,128)S(1)}, u32[]{:S(2)}, u32[]{:S(2)}) %collective-permute-start.7) | collective-permute-done | bytes 299040 | tf_op jit(solution)/shard_map/ppermute | solution.py:938
  33.8 2.9 %collective-permute-done.refs_1_ = f32[128,128]{1,0:T(8,128)S(1)} collective-permute-done((f32[128,128]{1,0:T(8,128)S(1)}, f32[128,128]{1,0:T(8,128)S(1)}, u32[]{:S(2)}, u32[]{:S(2)}) %collective-permute-start) | collective-permute-done | bytes 65568 | tf_op jit(solution)/shard_map/ppermute | solution.py:964
  38.4 2.8 %shard_map.85.field = f32[28,2,56,128]{3,2,1,0:T(8,128)S(1)} custom-call(s32[8]{0:T(128)S(1)} %stack.35.place, f32[28,2,56,128]{3,2,1,0:T(8,128)S(1)} %bitcast.12, f32[584,128]{1,0:T(8,128)S(1)} %collective-permute-done.3.low, f32[584,128]{1,0:T(8,128)S(1)} %collective-permute-done.4.high), custom_call_target="tpu_custom_call" | custom-call | flops 924844032 | bytes 1000000 | tf_op jit(solution)/shard_map/pallas_call | solution.py:213
  41.3 2.8 %shard_map.86.field = f32[28,2,56,128]{3,2,1,0:T(8,128)S(1)} custom-call(s32[8]{0:T(128)S(1)} %stack.35.place, f32[28,2,56,128]{3,2,1,0:T(8,128)S(1)} %shard_map.85.field, f32[584,128]{1,0:T(8,128)S(1)} %collective-permute-done.5.low, f32[584,128]{1,0:T(8,128)S(1)} %collective-permute-done.6.high), custom_call_target="tpu_custom_call" | custom-call | flops 924844032 | bytes 1000000 | tf_op jit(solution)/shard_map/pallas_call | solution.py:213
  45.4 11.3 %shard_map.87 = (f32[28,2,56,128]{3,2,1,0:T(8,128)S(1)}, f32[7,2,56,128]{3,2,1,0:T(8,128)S(1)}, f32[7,2,56,128]{3,2,1,0:T(8,128)S(1)}, f32[7,2,56,128]{3,2,1,0:T(8,128)S(1)}, f32[7,2,56,128]{3,2,1,0:T(8,128)S(1)}) custom-call(s32[8]{0:T(128)S(1)} %stack.35.place, f32[28,2,56,128]{3,2,1,0:T(8,128)S(1)} %bitcast.13, f32[28,2,56,128]{3,2,1,0:T(8,128)S(1)} %shard_map.86.field, ...), custom_call_target="tpu_custom_call" | custom-call | flops 3699376128 | bytes 1000000 | tf_op jit(solution)/shard_map/pallas_call | solution.py:302
  63.8 6.9 %collective-permute-done.9.refs_1_ = f32[7,2,56,128]{3,2,1,0:T(8,128)S(1)} collective-permute-done((f32[7,2,56,128]{3,2,1,0:T(8,128)S(1)}, f32[7,2,56,128]{3,2,1,0:T(8,128)S(1)}, u32[]{:S(2)}, u32[]{:S(2)}) %collective-permute-start.9) | collective-permute-done | bytes 401440 | tf_op jit(solution)/shard_map/ppermute | solution.py:964
  71.7 6.3 %collective-permute-done.11.refs_3_ = f32[7,2,56,128]{3,2,1,0:T(8,128)S(1)} collective-permute-done((f32[7,2,56,128]{3,2,1,0:T(8,128)S(1)}, f32[7,2,56,128]{3,2,1,0:T(8,128)S(1)}, u32[]{:S(2)}, u32[]{:S(2)}) %collective-permute-start.11) | collective-permute-done | bytes 401440 | tf_op jit(solution)/shard_map/ppermute | solution.py:964
  78.0 2.7 shard_map.88
  80.7 4.5 %collective-permute-start.12 = (f32[7,2,56,128]{3,2,1,0:T(8,128)S(1)}, f32[7,2,56,128]{3,2,1,0:T(8,128)S(1)}, u32[]{:S(2)}, u32[]{:S(2)}) collective-permute-start(f32[7,2,56,128]{3,2,1,0:T(8,128)S(1)} %shard_map.88), channel_id=1, source_target_pairs={{0,16},{4,20},{8,24},{12,28},{1,17},{5,21},{9,25},{13,29},{2,18},{... | collective-permute-start | bytes 1204232 | tf_op jit(solution)/shard_map/ppermute | solution.py:977
  88.1 5.9 %collective-permute-done.12.carry = f32[7,2,56,128]{3,2,1,0:T(8,128)S(1)} collective-permute-done((f32[7,2,56,128]{3,2,1,0:T(8,128)S(1)}, f32[7,2,56,128]{3,2,1,0:T(8,128)S(1)}, u32[]{:S(2)}, u32[]{:S(2)}) %collective-permute-start.12) | collective-permute-done | bytes 401440 | tf_op jit(solution)/shard_map/ppermute | solution.py:977
  94.7 10.0 %collective-permute-start.14 = (f32[7,2,56,128]{3,2,1,0:T(8,128)S(1)}, f32[7,2,56,128]{3,2,1,0:T(8,128)S(1)}, u32[]{:S(2)}, u32[]{:S(2)}) collective-permute-start(f32[7,2,56,128]{3,2,1,0:T(8,128)S(1)} %get-tuple-element.84), channel_id=1, source_target_pairs={{0,8},{4,12},{8,0},{12,4},{16,24},{20,28},{24,16},{28,20},{1,9},{5... | collective-permute-start | bytes 1204232 | tf_op jit(solution)/shard_map/ppermute | solution.py:964
  104.7 2.8 %collective-permute-start.15 = (f32[7,2,56,128]{3,2,1,0:T(8,128)S(1)}, f32[7,2,56,128]{3,2,1,0:T(8,128)S(1)}, u32[]{:S(2)}, u32[]{:S(2)}) collective-permute-start(f32[7,2,56,128]{3,2,1,0:T(8,128)S(1)} %get-tuple-element.85), channel_id=1, source_target_pairs={{0,12},{4,0},{8,4},{12,8},{16,28},{20,16},{24,20},{28,24},{1,13},{... | collective-permute-start | bytes 1204232 | tf_op jit(solution)/shard_map/ppermute | solution.py:964
  114.8 7.4 %collective-permute-done.15.refs_3_ = f32[7,2,56,128]{3,2,1,0:T(8,128)S(1)} collective-permute-done((f32[7,2,56,128]{3,2,1,0:T(8,128)S(1)}, f32[7,2,56,128]{3,2,1,0:T(8,128)S(1)}, u32[]{:S(2)}, u32[]{:S(2)}) %collective-permute-start.15) | collective-permute-done | bytes 401440 | tf_op jit(solution)/shard_map/ppermute | solution.py:964
  123.1 33.7 %shard_map.93 = (f32[28,2,56,128]{3,2,1,0:T(8,128)}, f32[28,2,56,128]{3,2,1,0:T(8,128)}, f32[28,2,56,128]{3,2,1,0:T(8,128)}, f32[28,2,56,128]{3,2,1,0:T(8,128)},...) custom-call(s32[8]{0:T(128)S(1)} %stack.35.place, ...), custom_call_target="tpu_custom_call" | custom-call | flops 11098128384 | bytes 1000000 | tf_op jit(solution)/shard_map/pallas_call | solution.py:667
  156.8 3.3 %collective-permute-start.20 = (f32[7,2,56,128]{3,2,1,0:T(8,128)S(1)}, f32[7,2,56,128]{3,2,1,0:T(8,128)S(1)}, u32[]{:S(2)}, u32[]{:S(2)}) collective-permute-start(f32[7,2,56,128]{3,2,1,0:T(8,128)S(1)} %get-tuple-element.95), channel_id=1, source_target_pairs={{28,24},{24,20},{20,16},{16,28},{12,8},{8,4},{4,0},{0,12},{29,25},... | collective-permute-start | bytes 1204232 | tf_op jit(solution)/shard_map/ppermute | solution.py:964
  161.9 8.0 %collective-permute-done.20.refs_1_ = f32[7,2,56,128]{3,2,1,0:T(8,128)S(1)} collective-permute-done((f32[7,2,56,128]{3,2,1,0:T(8,128)S(1)}, f32[7,2,56,128]{3,2,1,0:T(8,128)S(1)}, u32[]{:S(2)}, u32[]{:S(2)}) %collective-permute-start.20) | collective-permute-done | bytes 401440 | tf_op jit(solution)/shard_map/ppermute | solution.py:964
  169.9 8.1 %collective-permute-done.21.refs_2_ = f32[7,2,56,128]{3,2,1,0:T(8,128)S(1)} collective-permute-done((f32[7,2,56,128]{3,2,1,0:T(8,128)S(1)}, f32[7,2,56,128]{3,2,1,0:T(8,128)S(1)}, u32[]{:S(2)}, u32[]{:S(2)}) %collective-permute-start.21) | collective-permute-done | bytes 401440 | tf_op jit(solution)/shard_map/ppermute | solution.py:964
  179.2 2.7 shard_map.94
  185.5 18.3 %collective-permute-done.23.carry = f32[7,2,56,128]{3,2,1,0:T(8,128)S(1)} collective-permute-done((f32[7,2,56,128]{3,2,1,0:T(8,128)S(1)}, f32[7,2,56,128]{3,2,1,0:T(8,128)S(1)}, u32[]{:S(2)}, u32[]{:S(2)}) %collective-permute-start.23) | collective-permute-done | bytes 401440 | tf_op jit(solution)/shard_map/ppermute | solution.py:977
  208.2 7.5 %collective-permute-done.24.refs_1_ = f32[7,2,56,128]{3,2,1,0:T(8,128)S(1)} collective-permute-done((f32[7,2,56,128]{3,2,1,0:T(8,128)S(1)}, f32[7,2,56,128]{3,2,1,0:T(8,128)S(1)}, u32[]{:S(2)}, u32[]{:S(2)}) %collective-permute-start.24) | collective-permute-done | bytes 401440 | tf_op jit(solution)/shard_map/ppermute | solution.py:964
  215.7 8.6 %collective-permute-done.25.refs_2_ = f32[7,2,56,128]{3,2,1,0:T(8,128)S(1)} collective-permute-done((f32[7,2,56,128]{3,2,1,0:T(8,128)S(1)}, f32[7,2,56,128]{3,2,1,0:T(8,128)S(1)}, u32[]{:S(2)}, u32[]{:S(2)}) %collective-permute-start.25) | collective-permute-done | bytes 401440 | tf_op jit(solution)/shard_map/ppermute | solution.py:964
  224.5 4.3 %shard_map.98 = (f32[28,2,56,128]{3,2,1,0:T(8,128)S(1)}, f32[576,128]{1,0:T(8,128)S(1)}, f32[576,128]{1,0:T(8,128)S(1)}) custom-call(s32[8]{0:T(128)S(1)} %stack.35.place, f32[7,2,56,128]{3,2,1,0:T(8,128)S(1)} %get-tuple-element.100.refs_0_, f32[7,2,56,128]{3,2,1,0:T(8,128)S(1)} %collective-permute-done.24.refs_1_, ...), custom_call_target="tpu_custom_call" | custom-call | flops 924844032 | bytes 1000000 | tf_op jit(solution)/shard_map/pallas_call | solution.py:825
  230.6 6.0 %shard_map.100 = (f32[28,2,56,128]{3,2,1,0:T(8,128)S(1)}, f32[576,128]{1,0:T(8,128)S(1)}, f32[576,128]{1,0:T(8,128)S(1)}) custom-call(s32[8]{0:T(128)S(1)} %stack.35.place, f32[28,2,56,128]{3,2,1,0:T(8,128)S(1)} %get-tuple-element.106.adjoint.tops, f32[28,2,56,128]{3,2,1,0:T(8,128)S(1)} %copy-done.5, bf16[3,1152,128]{2,1,0:T(8,128)(2,1)S(1)} %copy-done.2, ...), custom_call_target="tpu_custom_call" | custom-call | flops 1849688064 | bytes 1000000 | tf_op jit(solution)/shard_map/pallas_call | solution.py:871
  240.0 6.0 %shard_map.102 = (f32[28,2,56,128]{3,2,1,0:T(8,128)S(1)}, f32[576,128]{1,0:T(8,128)S(1)}, f32[576,128]{1,0:T(8,128)S(1)}) custom-call(s32[8]{0:T(128)S(1)} %stack.35.place, f32[28,2,56,128]{3,2,1,0:T(8,128)S(1)} %get-tuple-element.112.adjoint, f32[28,2,56,128]{3,2,1,0:T(8,128)S(1)} %copy-done.3, bf16[3,1152,128]{2,1,0:T(8,128)(2,1)S(1)} %copy-done.2, ...), custom_call_target="tpu_custom_call" | custom-call | flops 1849688064 | bytes 1000000 | tf_op jit(solution)/shard_map/pallas_call | solution.py:871
  247.4 7.3 %collective-permute-done.31 = f32[576,128]{1,0:T(8,128)S(1)} collective-permute-done((f32[576,128]{1,0:T(8,128)S(1)}, f32[576,128]{1,0:T(8,128)S(1)}, u32[]{:S(2)}, u32[]{:S(2)}) %collective-permute-start.31) | collective-permute-done | bytes 294944 | tf_op jit(solution)/shard_map/ppermute | solution.py:942
  254.8 4.8 %shard_map.103 = (f32[28,2,56,128]{3,2,1,0:T(8,128)}, f32[28,2,56,128]{3,2,1,0:T(8,128)}) custom-call(f32[28,2,56,128]{3,2,1,0:T(8,128)S(1)} %get-tuple-element.120.adjoint, f32[28,2,56,128]{3,2,1,0:T(8,128)S(1)} %copy-done.4, bf16[3,1152,128]{2,1,0:T(8,128)(2,1)S(1)} %copy-done.2, f32[3,128]{1,0:T(4,128)S(1)} %copy-done.14, ...), custom_call_target="tpu_custom_call" | custom-call | flops 924844032 | bytes 1000000 | tf_op jit(solution)/shard_map/pallas_call | solution.py:902
  260.6 6.8 %collective-permute-done.32 = f32[576,128]{1,0:T(8,128)S(1)} collective-permute-done((f32[576,128]{1,0:T(8,128)S(1)}, f32[576,128]{1,0:T(8,128)S(1)}, u32[]{:S(2)}, u32[]{:S(2)}) %collective-permute-start.32) | collective-permute-done | bytes 294944 | tf_op jit(solution)/shard_map/ppermute | solution.py:942
  (113 shorter events, 53.3 us)
Async XLA Ops:
  3.3 12.5 %collective-permute-start.3 = (f32[584,128]{1,0:T(8,128)S(1)}, f32[584,128]{1,0:T(8,128)S(1)}, u32[]{:S(2)}, u32[]{:S(2)}) collective-permute-start(f32[584,128]{1,0:T(8,128)S(1)} %get-tuple-element.72), channel_id=1, source_target_pairs={{0,4},{4,8},{8,12},{12,16},{16,20},{20,24},{24,28},{1,5},{5,9},{9,... | collective-permute-start | bytes 897032 | tf_op jit(solution)/shard_map/ppermute | solution.py:938
  8.3 13.9 %collective-permute-start.5 = (f32[584,128]{1,0:T(8,128)S(1)}, f32[584,128]{1,0:T(8,128)S(1)}, u32[]{:S(2)}, u32[]{:S(2)}) collective-permute-start(f32[584,128]{1,0:T(8,128)S(1)} %get-tuple-element.73), channel_id=1, source_target_pairs={{0,4},{4,8},{8,12},{12,16},{16,20},{20,24},{24,28},{1,5},{5,9},{9,... | collective-permute-start | bytes 897032 | tf_op jit(solution)/shard_map/ppermute | solution.py:938
  11.8 17.1 %collective-permute-start.7 = (f32[584,128]{1,0:T(8,128)S(1)}, f32[584,128]{1,0:T(8,128)S(1)}, u32[]{:S(2)}, u32[]{:S(2)}) collective-permute-start(f32[584,128]{1,0:T(8,128)S(1)} %get-tuple-element.75), channel_id=1, source_target_pairs={{0,4},{4,8},{8,12},{12,16},{16,20},{20,24},{24,28},{1,5},{5,9},{9,... | collective-permute-start | bytes 897032 | tf_op jit(solution)/shard_map/ppermute | solution.py:938
  15.8 22.6 %collective-permute-start.4 = (f32[584,128]{1,0:T(8,128)S(1)}, f32[584,128]{1,0:T(8,128)S(1)}, u32[]{:S(2)}, u32[]{:S(2)}) collective-permute-start(f32[584,128]{1,0:T(8,128)S(1)} %collective-permute-done.3.low), channel_id=1, source_target_pairs={{0,1},{1,0},{2,3},{3,2},{4,5},{5,4},{6,7},{7,6},{8,9},{9,8},{10,11... | collective-permute-start | bytes 897032 | tf_op jit(solution)/shard_map/ppermute | solution.py:942
  22.2 19.0 %collective-permute-start.6 = (f32[584,128]{1,0:T(8,128)S(1)}, f32[584,128]{1,0:T(8,128)S(1)}, u32[]{:S(2)}, u32[]{:S(2)}) collective-permute-start(f32[584,128]{1,0:T(8,128)S(1)} %collective-permute-done.5.low), channel_id=1, source_target_pairs={{0,1},{1,0},{2,3},{3,2},{4,5},{5,4},{6,7},{7,6},{8,9},{9,8},{10,11... | collective-permute-start | bytes 897032 | tf_op jit(solution)/shard_map/ppermute | solution.py:942
  22.2 8.8 %collective-permute-start.2 = (f32[128,128]{1,0:T(8,128)S(1)}, f32[128,128]{1,0:T(8,128)S(1)}, u32[]{:S(2)}, u32[]{:S(2)}) collective-permute-start(f32[128,128]{1,0:T(8,128)S(1)} %get-tuple-element.68.refs_0_.matrix.refs_12_), channel_id=1, source_target_pairs={{0,12},{4,0},{8,4},{12,8},{16,28},{20,16},{24,20},{28,24},{1,13},{... | collective-permute-start | bytes 196616 | tf_op jit(solution)/shard_map/ppermute | solution.py:964
  28.9 16.5 %collective-permute-start.8 = (f32[584,128]{1,0:T(8,128)S(1)}, f32[584,128]{1,0:T(8,128)S(1)}, u32[]{:S(2)}, u32[]{:S(2)}) collective-permute-start(f32[584,128]{1,0:T(8,128)S(1)} %collective-permute-done.7.low), channel_id=1, source_target_pairs={{0,1},{1,0},{2,3},{3,2},{4,5},{5,4},{6,7},{7,6},{8,9},{9,8},{10,11... | collective-permute-start | bytes 897032 | tf_op jit(solution)/shard_map/ppermute | solution.py:942
  44.1 18.2 %collective-permute-start.16 = (f32[3,296,128]{2,1,0:T(8,128)S(1)}, f32[3,296,128]{2,1,0:T(8,128)S(1)}, u32[]{:S(2)}, u32[]{:S(2)}) collective-permute-start(f32[3,296,128]{2,1,0:T(8,128)S(1)} %get-tuple-element.87), channel_id=1, source_target_pairs={{4,0},{8,4},{12,8},{16,12},{20,16},{24,20},{28,24},{5,1},{9,5},{13... | collective-permute-start | bytes 1363976 | tf_op jit(solution)/shard_map/ppermute | solution.py:938
  56.7 13.9 %collective-permute-start.9 = (f32[7,2,56,128]{3,2,1,0:T(8,128)S(1)}, f32[7,2,56,128]{3,2,1,0:T(8,128)S(1)}, u32[]{:S(2)}, u32[]{:S(2)}) collective-permute-start(f32[7,2,56,128]{3,2,1,0:T(8,128)S(1)} %get-tuple-element.77), channel_id=1, source_target_pairs={{0,4},{4,8},{8,12},{12,0},{16,20},{20,24},{24,28},{28,16},{1,5},{5... | collective-permute-start | bytes 1204232 | tf_op jit(solution)/shard_map/ppermute | solution.py:964
  59.4 12.2 %collective-permute-start.10 = (f32[7,2,56,128]{3,2,1,0:T(8,128)S(1)}, f32[7,2,56,128]{3,2,1,0:T(8,128)S(1)}, u32[]{:S(2)}, u32[]{:S(2)}) collective-permute-start(f32[7,2,56,128]{3,2,1,0:T(8,128)S(1)} %get-tuple-element.78), channel_id=1, source_target_pairs={{0,8},{4,12},{8,0},{12,4},{16,24},{20,28},{24,16},{28,20},{1,9},{5... | collective-permute-start | bytes 1204232 | tf_op jit(solution)/shard_map/ppermute | solution.py:964
  61.0 16.9 %collective-permute-start.11 = (f32[7,2,56,128]{3,2,1,0:T(8,128)S(1)}, f32[7,2,56,128]{3,2,1,0:T(8,128)S(1)}, u32[]{:S(2)}, u32[]{:S(2)}) collective-permute-start(f32[7,2,56,128]{3,2,1,0:T(8,128)S(1)} %get-tuple-element.79), channel_id=1, source_target_pairs={{0,12},{4,0},{8,4},{12,8},{16,28},{20,16},{24,20},{28,24},{1,13},{... | collective-permute-start | bytes 1204232 | tf_op jit(solution)/shard_map/ppermute | solution.py:964
  62.3 23.0 %collective-permute-start.17 = (f32[3,296,128]{2,1,0:T(8,128)S(1)}, f32[3,296,128]{2,1,0:T(8,128)S(1)}, u32[]{:S(2)}, u32[]{:S(2)}) collective-permute-start(f32[3,296,128]{2,1,0:T(8,128)S(1)} %collective-permute-done.16.refs_0_), channel_id=1, source_target_pairs={{0,2},{1,3},{2,0},{3,1},{4,6},{5,7},{6,4},{7,5},{8,10},{9,11},{10,... | collective-permute-start | bytes 1363976 | tf_op jit(solution)/shard_map/ppermute | solution.py:942
  80.7 13.3 %collective-permute-start.12 = (f32[7,2,56,128]{3,2,1,0:T(8,128)S(1)}, f32[7,2,56,128]{3,2,1,0:T(8,128)S(1)}, u32[]{:S(2)}, u32[]{:S(2)}) collective-permute-start(f32[7,2,56,128]{3,2,1,0:T(8,128)S(1)} %shard_map.88), channel_id=1, source_target_pairs={{0,16},{4,20},{8,24},{12,28},{1,17},{5,21},{9,25},{13,29},{2,18},{... | collective-permute-start | bytes 1204232 | tf_op jit(solution)/shard_map/ppermute | solution.py:977
  85.2 23.6 %collective-permute-start.18 = (f32[3,296,128]{2,1,0:T(8,128)S(1)}, f32[3,296,128]{2,1,0:T(8,128)S(1)}, u32[]{:S(2)}, u32[]{:S(2)}) collective-permute-start(f32[3,296,128]{2,1,0:T(8,128)S(1)} %collective-permute-done.16.refs_0_), channel_id=1, source_target_pairs={{0,1},{1,0},{2,3},{3,2},{4,5},{5,4},{6,7},{7,6},{8,9},{9,8},{10,11... | collective-permute-start | bytes 1363976 | tf_op jit(solution)/shard_map/ppermute | solution.py:942
  85.3 23.5 %collective-permute-start.19 = (f32[3,296,128]{2,1,0:T(8,128)S(1)}, f32[3,296,128]{2,1,0:T(8,128)S(1)}, u32[]{:S(2)}, u32[]{:S(2)}) collective-permute-start(f32[3,296,128]{2,1,0:T(8,128)S(1)} %collective-permute-done.17.refs_1_), channel_id=1, source_target_pairs={{0,1},{1,0},{2,3},{3,2},{4,5},{5,4},{6,7},{7,6},{8,9},{9,8},{10,11... | collective-permute-start | bytes 1363976 | tf_op jit(solution)/shard_map/ppermute | solution.py:942
  94.6 19.8 %collective-permute-start.13 = (f32[7,2,56,128]{3,2,1,0:T(8,128)S(1)}, f32[7,2,56,128]{3,2,1,0:T(8,128)S(1)}, u32[]{:S(2)}, u32[]{:S(2)}) collective-permute-start(f32[7,2,56,128]{3,2,1,0:T(8,128)S(1)} %get-tuple-element.83), channel_id=1, source_target_pairs={{0,4},{4,8},{8,12},{12,0},{16,20},{20,24},{24,28},{28,16},{1,5},{5... | collective-permute-start | bytes 1204232 | tf_op jit(solution)/shard_map/ppermute | solution.py:964
  94.7 20.1 %collective-permute-start.14 = (f32[7,2,56,128]{3,2,1,0:T(8,128)S(1)}, f32[7,2,56,128]{3,2,1,0:T(8,128)S(1)}, u32[]{:S(2)}, u32[]{:S(2)}) collective-permute-start(f32[7,2,56,128]{3,2,1,0:T(8,128)S(1)} %get-tuple-element.84), channel_id=1, source_target_pairs={{0,8},{4,12},{8,0},{12,4},{16,24},{20,28},{24,16},{28,20},{1,9},{5... | collective-permute-start | bytes 1204232 | tf_op jit(solution)/shard_map/ppermute | solution.py:964
  104.7 17.5 %collective-permute-start.15 = (f32[7,2,56,128]{3,2,1,0:T(8,128)S(1)}, f32[7,2,56,128]{3,2,1,0:T(8,128)S(1)}, u32[]{:S(2)}, u32[]{:S(2)}) collective-permute-start(f32[7,2,56,128]{3,2,1,0:T(8,128)S(1)} %get-tuple-element.85), channel_id=1, source_target_pairs={{0,12},{4,0},{8,4},{12,8},{16,28},{20,16},{24,20},{28,24},{1,13},{... | collective-permute-start | bytes 1204232 | tf_op jit(solution)/shard_map/ppermute | solution.py:964
  156.8 13.1 %collective-permute-start.20 = (f32[7,2,56,128]{3,2,1,0:T(8,128)S(1)}, f32[7,2,56,128]{3,2,1,0:T(8,128)S(1)}, u32[]{:S(2)}, u32[]{:S(2)}) collective-permute-start(f32[7,2,56,128]{3,2,1,0:T(8,128)S(1)} %get-tuple-element.95), channel_id=1, source_target_pairs={{28,24},{24,20},{20,16},{16,28},{12,8},{8,4},{4,0},{0,12},{29,25},... | collective-permute-start | bytes 1204232 | tf_op jit(solution)/shard_map/ppermute | solution.py:964
  160.1 17.9 %collective-permute-start.21 = (f32[7,2,56,128]{3,2,1,0:T(8,128)S(1)}, f32[7,2,56,128]{3,2,1,0:T(8,128)S(1)}, u32[]{:S(2)}, u32[]{:S(2)}) collective-permute-start(f32[7,2,56,128]{3,2,1,0:T(8,128)S(1)} %get-tuple-element.96), channel_id=1, source_target_pairs={{28,20},{24,16},{20,28},{16,24},{12,4},{8,0},{4,12},{0,8},{29,21},... | collective-permute-start | bytes 1204232 | tf_op jit(solution)/shard_map/ppermute | solution.py:964
  160.3 18.9 %collective-permute-start.22 = (f32[7,2,56,128]{3,2,1,0:T(8,128)S(1)}, f32[7,2,56,128]{3,2,1,0:T(8,128)S(1)}, u32[]{:S(2)}, u32[]{:S(2)}) collective-permute-start(f32[7,2,56,128]{3,2,1,0:T(8,128)S(1)} %get-tuple-element.97), channel_id=1, source_target_pairs={{28,16},{24,28},{20,24},{16,20},{12,0},{8,12},{4,8},{0,4},{29,17},... | collective-permute-start | bytes 1204232 | tf_op jit(solution)/shard_map/ppermute | solution.py:964
  181.9 21.9 %collective-permute-start.23 = (f32[7,2,56,128]{3,2,1,0:T(8,128)S(1)}, f32[7,2,56,128]{3,2,1,0:T(8,128)S(1)}, u32[]{:S(2)}, u32[]{:S(2)}) collective-permute-start(f32[7,2,56,128]{3,2,1,0:T(8,128)S(1)} %shard_map.94), channel_id=1, source_target_pairs={{28,12},{24,8},{20,4},{16,0},{29,13},{25,9},{21,5},{17,1},{30,14},... | collective-permute-start | bytes 1204232 | tf_op jit(solution)/shard_map/ppermute | solution.py:977
  204.4 11.4 %collective-permute-start.24 = (f32[7,2,56,128]{3,2,1,0:T(8,128)S(1)}, f32[7,2,56,128]{3,2,1,0:T(8,128)S(1)}, u32[]{:S(2)}, u32[]{:S(2)}) collective-permute-start(f32[7,2,56,128]{3,2,1,0:T(8,128)S(1)} %get-tuple-element.101), channel_id=1, source_target_pairs={{28,24},{24,20},{20,16},{16,28},{12,8},{8,4},{4,0},{0,12},{29,25},... | collective-permute-start | bytes 1204232 | tf_op jit(solution)/shard_map/ppermute | solution.py:964
  204.4 19.9 %collective-permute-start.25 = (f32[7,2,56,128]{3,2,1,0:T(8,128)S(1)}, f32[7,2,56,128]{3,2,1,0:T(8,128)S(1)}, u32[]{:S(2)}, u32[]{:S(2)}) collective-permute-start(f32[7,2,56,128]{3,2,1,0:T(8,128)S(1)} %get-tuple-element.102), channel_id=1, source_target_pairs={{28,20},{24,16},{20,28},{16,24},{12,4},{8,0},{4,12},{0,8},{29,21},... | collective-permute-start | bytes 1204232 | tf_op jit(solution)/shard_map/ppermute | solution.py:964
  207.0 17.5 %collective-permute-start.26 = (f32[7,2,56,128]{3,2,1,0:T(8,128)S(1)}, f32[7,2,56,128]{3,2,1,0:T(8,128)S(1)}, u32[]{:S(2)}, u32[]{:S(2)}) collective-permute-start(f32[7,2,56,128]{3,2,1,0:T(8,128)S(1)} %get-tuple-element.103), channel_id=1, source_target_pairs={{28,16},{24,28},{20,24},{16,20},{12,0},{8,12},{4,8},{0,4},{29,17},... | collective-permute-start | bytes 1204232 | tf_op jit(solution)/shard_map/ppermute | solution.py:964
  228.8 9.5 %collective-permute-start.27 = (f32[576,128]{1,0:T(8,128)S(1)}, f32[576,128]{1,0:T(8,128)S(1)}, u32[]{:S(2)}, u32[]{:S(2)}) collective-permute-start(f32[576,128]{1,0:T(8,128)S(1)} %get-tuple-element.111), channel_id=1, source_target_pairs={{0,1},{1,0},{2,3},{3,2},{4,5},{5,4},{6,7},{7,6},{8,9},{9,8},{10,11... | collective-permute-start | bytes 884744 | tf_op jit(solution)/shard_map/ppermute | solution.py:942
  236.6 9.4 %collective-permute-start.28 = (f32[576,128]{1,0:T(8,128)S(1)}, f32[576,128]{1,0:T(8,128)S(1)}, u32[]{:S(2)}, u32[]{:S(2)}) collective-permute-start(f32[576,128]{1,0:T(8,128)S(1)} %get-tuple-element.117), channel_id=1, source_target_pairs={{0,1},{1,0},{2,3},{3,2},{4,5},{5,4},{6,7},{7,6},{8,9},{9,8},{10,11... | collective-permute-start | bytes 884744 | tf_op jit(solution)/shard_map/ppermute | solution.py:942
  238.4 9.0 %collective-permute-start.29 = (f32[576,128]{1,0:T(8,128)S(1)}, f32[576,128]{1,0:T(8,128)S(1)}, u32[]{:S(2)}, u32[]{:S(2)}) collective-permute-start(f32[576,128]{1,0:T(8,128)S(1)} %add.18), channel_id=1, source_target_pairs={{0,2},{1,3},{2,0},{3,1},{4,6},{5,7},{6,4},{7,5},{8,10},{9,11},{10,... | collective-permute-start | bytes 884744 | tf_op jit(solution)/shard_map/ppermute | solution.py:942
  246.0 8.7 %collective-permute-start.31 = (f32[576,128]{1,0:T(8,128)S(1)}, f32[576,128]{1,0:T(8,128)S(1)}, u32[]{:S(2)}, u32[]{:S(2)}) collective-permute-start(f32[576,128]{1,0:T(8,128)S(1)} %add.19), channel_id=1, source_target_pairs={{0,2},{1,3},{2,0},{3,1},{4,6},{5,7},{6,4},{7,5},{8,10},{9,11},{10,... | collective-permute-start | bytes 884744 | tf_op jit(solution)/shard_map/ppermute | solution.py:942
  246.6 13.0 %collective-permute-start.30 = (f32[576,128]{1,0:T(8,128)S(1)}, f32[576,128]{1,0:T(8,128)S(1)}, u32[]{:S(2)}, u32[]{:S(2)}) collective-permute-start(f32[576,128]{1,0:T(8,128)S(1)} %get-tuple-element.124), channel_id=1, source_target_pairs={{0,1},{1,0},{2,3},{3,2},{4,5},{5,4},{6,7},{7,6},{8,9},{9,8},{10,11... | collective-permute-start | bytes 884744 | tf_op jit(solution)/shard_map/ppermute | solution.py:942
  259.6 7.8 %collective-permute-start.32 = (f32[576,128]{1,0:T(8,128)S(1)}, f32[576,128]{1,0:T(8,128)S(1)}, u32[]{:S(2)}, u32[]{:S(2)}) collective-permute-start(f32[576,128]{1,0:T(8,128)S(1)} %add.21), channel_id=1, source_target_pairs={{0,2},{1,3},{2,0},{3,1},{4,6},{5,7},{6,4},{7,5},{8,10},{9,11},{10,... | collective-permute-start | bytes 884744 | tf_op jit(solution)/shard_map/ppermute | solution.py:942
  260.1 7.4 %collective-permute-start.34 = (f32[576,128]{1,0:T(8,128)S(1)}, f32[576,128]{1,0:T(8,128)S(1)}, u32[]{:S(2)}, u32[]{:S(2)}) collective-permute-start(f32[576,128]{1,0:T(8,128)S(1)} %add.22.refs_2_), channel_id=1, source_target_pairs={{0,1},{1,0},{2,3},{3,2},{4,5},{5,4},{6,7},{7,6},{8,9},{9,8},{10,11... | collective-permute-start | bytes 884744 | tf_op jit(solution)/shard_map/ppermute | solution.py:942
  (26 other events, 243.6 us)
